TPU v7x, 32 devices: a whole 2x2x4 slice. The times are simulated.
32 devices in a mesh: rep: 4 (over x, core), shard: 4 (over z), ctx: 2 (over y).
Axes of the slice: x: 2, y: 2, z: 4, core: 2. Of those that a mesh axis runs over, the one named last changes fastest.
Arguments:
- tokens: bfloat16 [16, 1024, 512], P(('rep', 'shard'), 'ctx'), may hold values from -6 to 6
- encoded: bfloat16 [16, 512, 512], P(('rep', 'shard'), 'ctx'), may hold values from -6 to 6
- positions: int32 [16, 1024], P(('rep', 'shard'), 'ctx'), may hold values from 0 to 1023, as said below
- bucket_table: int32 [1024], replicated, may hold values from 0 to 31, never falling along the last dimension, each value on 1 to 128 neighbouring positions
- gain_self: bfloat16 [512], P('shard'), may hold values from 0.5 to 1.5
- w_query: bfloat16 [512, 384], P('shard'), may hold values from -0.125 to 0.125
- w_key: bfloat16 [512, 384], P('shard'), may hold values from -0.125 to 0.125
- w_value: bfloat16 [512, 384], P('shard'), may hold values from -0.25 to 0.25
- w_out: bfloat16 [384, 512], P('shard'), may hold values from -1.25 to 1.25
- bias_table: bfloat16 [32, 6], P('shard'), may hold values from -4 to 4
- gain_cross: bfloat16 [512], P('shard'), may hold values from 0.5 to 1.5
- c_query: bfloat16 [512, 384], P('shard'), may hold values from -0.125 to 0.125
- c_key: bfloat16 [512, 384], P('shard'), may hold values from -0.125 to 0.125
- c_value: bfloat16 [512, 384], P('shard'), may hold values from -0.25 to 0.25
- c_out: bfloat16 [384, 512], P('shard'), may hold values from -1.25 to 1.25
- gain_ff: bfloat16 [512], P('shard'), may hold values from 0.5 to 1.5
- w_gate: bfloat16 [512, 1024], P('shard'), may hold values from -0.25 to 0.25
- w_up: bfloat16 [512, 1024], P('shard'), may hold values from -0.25 to 0.25
- w_down: bfloat16 [1024, 512], P('shard'), may hold values from -0.25 to 0.25
- cotangent: bfloat16 [16, 1024, 512], P(('rep', 'shard'), 'ctx'), may hold values from -6 to 6
Outputs:
- layer_output: bfloat16 [16, 1024, 512], P(('rep', 'shard'), 'ctx')
- tokens_grad: float32 [16, 1024, 512], P(('rep', 'shard'), 'ctx')
- encoded_grad: float32 [16, 512, 512], P(('rep', 'shard'), 'ctx')
- grad_gain_self: float32 [512], P('shard')
- grad_w_query: float32 [512, 384], P('shard')
- grad_w_key: float32 [512, 384], P('shard')
- grad_w_value: float32 [512, 384], P('shard')
- grad_w_out: float32 [384, 512], P('shard')
- grad_bias_table: float32 [32, 6], P('shard')
- grad_gain_cross: float32 [512], P('shard')
- grad_c_query: float32 [512, 384], P('shard')
- grad_c_key: float32 [512, 384], P('shard')
- grad_c_value: float32 [512, 384], P('shard')
- grad_c_out: float32 [384, 512], P('shard')
- grad_gain_ff: float32 [512], P('shard')
- grad_w_gate: float32 [512, 1024], P('shard')
- grad_w_up: float32 [512, 1024], P('shard')
- grad_w_down: float32 [1024, 512], P('shard')
Inputs may be any that keep to these rules, and one draw needn't show every extreme that they name: In each sequence every position of 0 to 1023 stands in exactly one slot, and each aligned run of 64 slots holds 64 consecutive positions in increasing order. `bucket_table`: never falls as the offset grows; each bucket holds 1 to 128 offsets.
All inputs are finite; a program needn't handle non-finite values.
Results may differ from a plain program's by a relative error of at most 0.033.
The roundings to bfloat16 on the way count: a program that leaves them out, or rounds other values in their place, can miss the bound.
Values may be sent and summed in bfloat16 or wider, within the bound.
A program may use at most 192 MiB of HBM per device.

v0:
```python
import jax
import jax.numpy as jnp
from jax import lax
from jax.sharding import PartitionSpec as P

HEADS = 6
DH = 64
NB = 32


epsilon = 1e-06
masked_value = -1e30


def rms_norm(inputs, gain):
    return inputs * lax.rsqrt(jnp.mean(inputs * inputs, axis=-1, keepdims=True) + epsilon) * gain


def gated_gelu(gate, upper):
    return jax.nn.gelu(gate, approximate=True) * upper


def product(left, right):
    return jnp.dot(left, right, preferred_element_type=jnp.float32)


def left_matrix_product(left, right):
    return lax.dot_general(
        left, right, (((0,), (0,)), ((), ())), preferred_element_type=jnp.float32
    )


def right_product(left, right):
    return lax.dot_general(
        left, right, (((1,), (1,)), ((), ())), preferred_element_type=jnp.float32
    )


def split_heads(value):
    return value.reshape(value.shape[0], HEADS, DH)


def raw_scores(query, keys):
    return jnp.einsum(
        "qhd,khd->hqk", split_heads(query), split_heads(keys), preferred_element_type=jnp.float32
    )


def mix_values(probs, values):
    mixed = jnp.einsum(
        "hqk,khd->qhd",
        probs.astype(jnp.bfloat16),
        split_heads(values),
        preferred_element_type=jnp.float32,
    )
    return mixed.reshape(mixed.shape[0], HEADS * DH).astype(jnp.bfloat16)


def bucket_starts(bucket_table):
    levels = jnp.arange(NB + 1, dtype=jnp.int32)
    return jnp.sum((bucket_table[:, None] < levels[None, :]).astype(jnp.int32), axis=0)


def bucket_ids(offsets, starts):
    inner_starts = starts[1:NB]
    return jnp.sum((offsets[None] >= inner_starts[:, None, None]).astype(jnp.int32), axis=0)


def bucket_bias(offsets, starts, table):
    ids = bucket_ids(offsets, starts)
    levels = jnp.arange(NB, dtype=jnp.int32)
    chosen = ids[None, None] == levels[:, None, None, None]
    return jnp.sum(jnp.where(chosen, table[:, :, None, None], 0.0), axis=0)


def bucket_grad(score_grad, offsets, starts):
    ids = bucket_ids(offsets, starts)
    levels = jnp.arange(NB, dtype=jnp.int32)
    chosen = ids[None, None] == levels[:, None, None, None]
    return jnp.sum(jnp.where(chosen, score_grad[None].astype(jnp.float32), 0.0), axis=(2, 3))


def score_grads(probs, grad_out, values, delta):
    grad_probs = jnp.einsum(
        "qhd,khd->hqk",
        split_heads(grad_out),
        split_heads(values),
        preferred_element_type=jnp.float32,
    )
    delta = jnp.sum(probs * grad_probs, axis=-1)
    return ((probs * (grad_probs - delta[..., None])).astype(jnp.bfloat16), delta)


def query_grad_of(grad_scores, keys):
    query_grad = jnp.einsum(
        "hqk,khd->qhd", grad_scores, split_heads(keys), preferred_element_type=jnp.float32
    )
    return query_grad.reshape(query_grad.shape[0], HEADS * DH).astype(jnp.bfloat16)


def key_terms(grad_scores, probs, query, grad_out):
    key_term = jnp.einsum(
        "hqk,qhd->khd", grad_scores, split_heads(query), preferred_element_type=jnp.float32
    )
    value_term = jnp.einsum(
        "hqk,qhd->khd",
        probs.astype(jnp.bfloat16),
        split_heads(grad_out),
        preferred_element_type=jnp.float32,
    )
    count = key_term.shape[0]
    return (key_term.reshape(count, HEADS * DH), value_term.reshape(count, HEADS * DH))


def local(
    tokens,
    encoded,
    positions,
    bucket_table,
    gain_self,
    w_query,
    w_key,
    w_value,
    w_out,
    bias_table,
    gain_cross,
    c_query,
    c_key,
    c_value,
    c_out,
    gain_ff,
    w_gate,
    w_up,
    w_down,
    cotangent,
):
    owned = (
        gain_self,
        w_query,
        w_key,
        w_value,
        w_out,
        bias_table,
        gain_cross,
        c_query,
        c_key,
        c_value,
        c_out,
        gain_ff,
        w_gate,
        w_up,
        w_down,
    )
    gathered = (
        lax.all_gather(owned[0], "shard", axis=0, tiled=True),
        lax.all_gather(owned[1], "shard", axis=0, tiled=True),
        lax.all_gather(owned[2], "shard", axis=0, tiled=True),
        lax.all_gather(owned[3], "shard", axis=0, tiled=True),
        lax.all_gather(owned[4], "shard", axis=0, tiled=True),
        lax.all_gather(owned[5], "shard", axis=0, tiled=True),
        lax.all_gather(owned[6], "shard", axis=0, tiled=True),
        lax.all_gather(owned[7], "shard", axis=0, tiled=True),
        lax.all_gather(owned[8], "shard", axis=0, tiled=True),
        lax.all_gather(owned[9], "shard", axis=0, tiled=True),
        lax.all_gather(owned[10], "shard", axis=0, tiled=True),
        lax.all_gather(owned[11], "shard", axis=0, tiled=True),
        lax.all_gather(owned[12], "shard", axis=0, tiled=True),
        lax.all_gather(owned[13], "shard", axis=0, tiled=True),
        lax.all_gather(owned[14], "shard", axis=0, tiled=True),
    )
    (
        self_gain,
        self_query,
        self_key,
        self_value,
        self_out,
        table_full,
        cross_gain,
        cross_query,
        cross_key,
        cross_value,
        cross_out,
        feed_gain,
        feed_gate,
        feed_up,
        feed_down,
    ) = gathered
    inputs = tokens[0].astype(jnp.float32)
    encoder = encoded[0]
    local_pos = positions[0]
    all_pos = lax.all_gather(local_pos, "ctx", axis=0, tiled=True)
    offsets = local_pos[:, None] - all_pos[None, :]
    causal = offsets >= 0
    starts = bucket_starts(bucket_table)
    table_value = table_full.astype(jnp.float32)
    bias = bucket_bias(offsets, starts, table_value)
    gain_one = self_gain.astype(jnp.float32)
    hidden_first_layer = rms_norm(inputs, gain_one).astype(jnp.bfloat16)
    query = product(hidden_first_layer, self_query).astype(jnp.bfloat16)
    keys = product(hidden_first_layer, self_key).astype(jnp.bfloat16)
    values = product(hidden_first_layer, self_value).astype(jnp.bfloat16)
    enc_keys = product(encoder, cross_key).astype(jnp.bfloat16)
    encoder_value_rows = product(encoder, cross_value).astype(jnp.bfloat16)
    all_keys, all_values, all_enc_keys, all_enc_values = (
        lax.all_gather(keys, "ctx", axis=0, tiled=True),
        lax.all_gather(values, "ctx", axis=0, tiled=True),
        lax.all_gather(enc_keys, "ctx", axis=0, tiled=True),
        lax.all_gather(encoder_value_rows, "ctx", axis=0, tiled=True),
    )

    def self_scores():
        return jnp.where(causal[None], raw_scores(query, all_keys) + bias, masked_value)

    scores_one = self_scores()
    lse_one = jax.nn.logsumexp(scores_one, axis=-1)
    attn_one = mix_values(jnp.exp(scores_one - lse_one[..., None]), all_values)
    after_one = inputs + product(attn_one, self_out)
    gain_two = cross_gain.astype(jnp.float32)
    hidden_two = rms_norm(after_one, gain_two).astype(jnp.bfloat16)
    cross_q = product(hidden_two, cross_query).astype(jnp.bfloat16)
    scores_two = raw_scores(cross_q, all_enc_keys)
    lse_two = jax.nn.logsumexp(scores_two, axis=-1)
    attn_two = mix_values(jnp.exp(scores_two - lse_two[..., None]), all_enc_values)
    after_two = after_one + product(attn_two, cross_out)
    gain_three = feed_gain.astype(jnp.float32)
    hidden_three = rms_norm(after_two, gain_three).astype(jnp.bfloat16)
    gate = product(hidden_three, feed_gate)
    upper = product(hidden_three, feed_up)
    mixed = gated_gelu(gate, upper).astype(jnp.bfloat16)
    decoder_output = (after_two + product(mixed, feed_down)).astype(jnp.bfloat16)
    regathered = (
        lax.all_gather(owned[0], "shard", axis=0, tiled=True),
        lax.all_gather(owned[1], "shard", axis=0, tiled=True),
        lax.all_gather(owned[2], "shard", axis=0, tiled=True),
        lax.all_gather(owned[3], "shard", axis=0, tiled=True),
        lax.all_gather(owned[4], "shard", axis=0, tiled=True),
        lax.all_gather(owned[5], "shard", axis=0, tiled=True),
        lax.all_gather(owned[6], "shard", axis=0, tiled=True),
        lax.all_gather(owned[7], "shard", axis=0, tiled=True),
        lax.all_gather(owned[8], "shard", axis=0, tiled=True),
        lax.all_gather(owned[9], "shard", axis=0, tiled=True),
        lax.all_gather(owned[10], "shard", axis=0, tiled=True),
        lax.all_gather(owned[11], "shard", axis=0, tiled=True),
        lax.all_gather(owned[12], "shard", axis=0, tiled=True),
        lax.all_gather(owned[13], "shard", axis=0, tiled=True),
        lax.all_gather(owned[14], "shard", axis=0, tiled=True),
    )
    (
        self_gain,
        self_query,
        self_key,
        self_value,
        self_out,
        table_full,
        cross_gain,
        cross_query,
        cross_key,
        cross_value,
        cross_out,
        feed_gain,
        feed_gate,
        feed_up,
        feed_down,
    ) = regathered
    grad_res = cotangent[0].astype(jnp.float32)
    grad_low = grad_res.astype(jnp.bfloat16)
    down_grad = left_matrix_product(mixed, grad_low)
    mixed_grad = right_product(grad_low, feed_down)
    unused, gelu_pull = jax.vjp(gated_gelu, gate, upper)
    gate_grad, upper_grad = gelu_pull(mixed_grad)
    gate_grad = gate_grad.astype(jnp.bfloat16)
    upper_grad = upper_grad.astype(jnp.bfloat16)
    wgate_grad = left_matrix_product(hidden_three, gate_grad)
    wup_grad = left_matrix_product(hidden_three, upper_grad)
    hidden_grad = right_product(gate_grad, feed_gate) + right_product(upper_grad, feed_up)
    unused, norm_pull = jax.vjp(rms_norm, after_two, gain_three)
    back_three, feed_gain_grad = norm_pull(hidden_grad)
    grad_two = grad_res + back_three
    cross_low = grad_two.astype(jnp.bfloat16)
    cross_output_grad = left_matrix_product(attn_two, cross_low)
    attn_two_grad = right_product(cross_low, cross_out).astype(jnp.bfloat16)
    probs_two = jnp.exp(raw_scores(cross_q, all_enc_keys) - lse_two[..., None])
    cross_scores_grad, delta_two = score_grads(probs_two, attn_two_grad, all_enc_values, None)
    cq_grad = query_grad_of(cross_scores_grad, all_enc_keys)
    cquery_grad = left_matrix_product(hidden_two, cq_grad)
    hidden_grad = right_product(cq_grad, cross_query)
    unused, norm_pull = jax.vjp(rms_norm, after_one, gain_two)
    back_two, cross_gain_grad = norm_pull(hidden_grad)
    grad_one = grad_two + back_two
    self_low = grad_one.astype(jnp.bfloat16)
    sout_grad = left_matrix_product(attn_one, self_low)
    attn_one_grad = right_product(self_low, self_out).astype(jnp.bfloat16)
    probs_one = jnp.exp(self_scores() - lse_one[..., None])
    self_scores_grad, delta_one = score_grads(probs_one, attn_one_grad, all_values, None)
    query_grad = query_grad_of(self_scores_grad, all_keys)
    table_grad = bucket_grad(self_scores_grad, offsets, starts)
    key_term, value_term = key_terms(self_scores_grad, probs_one, query, attn_one_grad)
    enckey_term, encvalue_term = key_terms(cross_scores_grad, probs_two, cross_q, attn_two_grad)
    key_sum, value_sum, enckey_sum, encvalue_sum = (
        lax.psum_scatter(
            key_term.astype(jnp.bfloat16), "ctx", scatter_dimension=0, tiled=True
        ).astype(jnp.float32),
        lax.psum_scatter(
            value_term.astype(jnp.bfloat16), "ctx", scatter_dimension=0, tiled=True
        ).astype(jnp.float32),
        lax.psum_scatter(
            enckey_term.astype(jnp.bfloat16), "ctx", scatter_dimension=0, tiled=True
        ).astype(jnp.float32),
        lax.psum_scatter(
            encvalue_term.astype(jnp.bfloat16), "ctx", scatter_dimension=0, tiled=True
        ).astype(jnp.float32),
    )
    key_reduced_precision = key_sum.astype(jnp.bfloat16)
    value_low = value_sum.astype(jnp.bfloat16)
    enckey_low = enckey_sum.astype(jnp.bfloat16)
    encvalue_low = encvalue_sum.astype(jnp.bfloat16)
    squery_grad = left_matrix_product(hidden_first_layer, query_grad)
    self_key_gradient = left_matrix_product(hidden_first_layer, key_reduced_precision)
    svalue_grad = left_matrix_product(hidden_first_layer, value_low)
    hidden_grad = (
        right_product(query_grad, self_query)
        + right_product(key_reduced_precision, self_key)
        + right_product(value_low, self_value)
    )
    unused, norm_pull = jax.vjp(rms_norm, inputs, gain_one)
    back_one, self_gain_grad = norm_pull(hidden_grad)
    input_grad = grad_one + back_one
    encoder_grad = right_product(enckey_low, cross_key) + right_product(encvalue_low, cross_value)
    ckey_grad = left_matrix_product(encoder, enckey_low)
    cvalue_grad = left_matrix_product(encoder, encvalue_low)
    local_grads = (
        self_gain_grad,
        squery_grad,
        self_key_gradient,
        svalue_grad,
        sout_grad,
        table_grad,
        cross_gain_grad,
        cquery_grad,
        ckey_grad,
        cvalue_grad,
        cross_output_grad,
        feed_gain_grad,
        wgate_grad,
        wup_grad,
        down_grad,
    )
    owned_grads = (
        lax.psum_scatter(
            local_grads[0].astype(jnp.bfloat16), "shard", scatter_dimension=0, tiled=True
        ).astype(jnp.float32),
        lax.psum_scatter(
            local_grads[1].astype(jnp.bfloat16), "shard", scatter_dimension=0, tiled=True
        ).astype(jnp.float32),
        lax.psum_scatter(
            local_grads[2].astype(jnp.bfloat16), "shard", scatter_dimension=0, tiled=True
        ).astype(jnp.float32),
        lax.psum_scatter(
            local_grads[3].astype(jnp.bfloat16), "shard", scatter_dimension=0, tiled=True
        ).astype(jnp.float32),
        lax.psum_scatter(
            local_grads[4].astype(jnp.bfloat16), "shard", scatter_dimension=0, tiled=True
        ).astype(jnp.float32),
        lax.psum_scatter(
            local_grads[5].astype(jnp.bfloat16), "shard", scatter_dimension=0, tiled=True
        ).astype(jnp.float32),
        lax.psum_scatter(
            local_grads[6].astype(jnp.bfloat16), "shard", scatter_dimension=0, tiled=True
        ).astype(jnp.float32),
        lax.psum_scatter(
            local_grads[7].astype(jnp.bfloat16), "shard", scatter_dimension=0, tiled=True
        ).astype(jnp.float32),
        lax.psum_scatter(
            local_grads[8].astype(jnp.bfloat16), "shard", scatter_dimension=0, tiled=True
        ).astype(jnp.float32),
        lax.psum_scatter(
            local_grads[9].astype(jnp.bfloat16), "shard", scatter_dimension=0, tiled=True
        ).astype(jnp.float32),
        lax.psum_scatter(
            local_grads[10].astype(jnp.bfloat16), "shard", scatter_dimension=0, tiled=True
        ).astype(jnp.float32),
        lax.psum_scatter(
            local_grads[11].astype(jnp.bfloat16), "shard", scatter_dimension=0, tiled=True
        ).astype(jnp.float32),
        lax.psum_scatter(
            local_grads[12].astype(jnp.bfloat16), "shard", scatter_dimension=0, tiled=True
        ).astype(jnp.float32),
        lax.psum_scatter(
            local_grads[13].astype(jnp.bfloat16), "shard", scatter_dimension=0, tiled=True
        ).astype(jnp.float32),
        lax.psum_scatter(
            local_grads[14].astype(jnp.bfloat16), "shard", scatter_dimension=0, tiled=True
        ).astype(jnp.float32),
    )
    summed = lax.psum(
        (
            owned_grads[0],
            owned_grads[1],
            owned_grads[2],
            owned_grads[3],
            owned_grads[4],
            owned_grads[5],
            owned_grads[6],
            owned_grads[7],
            owned_grads[8],
            owned_grads[9],
            owned_grads[10],
            owned_grads[11],
            owned_grads[12],
            owned_grads[13],
            owned_grads[14],
        ),
        ("rep", "ctx"),
    )
    return (
        decoder_output[None],
        input_grad[None],
        encoder_grad[None],
        summed[0],
        summed[1],
        summed[2],
        summed[3],
        summed[4],
        summed[5],
        summed[6],
        summed[7],
        summed[8],
        summed[9],
        summed[10],
        summed[11],
        summed[12],
        summed[13],
        summed[14],
    )


def solution(mesh):
    return jax.shard_map(
        local,
        mesh=mesh,
        in_specs=(
            P(("rep", "shard"), "ctx", None),
            P(("rep", "shard"), "ctx", None),
            P(("rep", "shard"), "ctx"),
            P(),
            P("shard"),
            P("shard", None),
            P("shard", None),
            P("shard", None),
            P("shard", None),
            P("shard", None),
            P("shard"),
            P("shard", None),
            P("shard", None),
            P("shard", None),
            P("shard", None),
            P("shard"),
            P("shard", None),
            P("shard", None),
            P("shard", None),
            P(("rep", "shard"), "ctx", None),
        ),
        out_specs=(
            P(("rep", "shard"), "ctx", None),
            P(("rep", "shard"), "ctx", None),
            P(("rep", "shard"), "ctx", None),
            P("shard"),
            P("shard", None),
            P("shard", None),
            P("shard", None),
            P("shard", None),
            P("shard", None),
            P("shard"),
            P("shard", None),
            P("shard", None),
            P("shard", None),
            P("shard", None),
            P("shard"),
            P("shard", None),
            P("shard", None),
            P("shard", None),
        ),
        check_vma=False,
    )
```

profile of v0, /device:TPU:1, one launch (start us, length us, event | category | flops | bytes accessed | tf_op | source)
XLA Modules:
  0.0 856.9 jit_solution(17975575864435049180)
XLA Ops:
  9.5 4.0 all-gather
  18.4 9.6 %all-gather.1 = bf16[4,1,128]{2,1,0:T(2,128)(2,1)S(1)} all-gather(bf16[1,1,128]{2,1,0:T(2,128)(2,1)} %bitcast.227), channel_id=1, replica_groups=mesh['rep'=4,'shard'=4,'ctx'=2] {'shard'}, dimensions={0}, use_global_device_ids=true | all-gather | bytes 1280 | tf_op jit(solution)/shard_map/all_gather | solution.py:155
  28.1 6.2 all-gather.2
  34.2 9.4 %all_gather.78 = bf16[32,6]{1,0:T(8,128)(2,1)S(1)} all-gather(bf16[8,6]{1,0:T(8,128)(2,1)} %param.29), channel_id=1, replica_groups=mesh['rep'=4,'shard'=4,'ctx'=2] {'shard'}, dimensions={0}, use_global_device_ids=true | all-gather | bytes 480 | tf_op jit(solution)/shard_map/all_gather | solution.py:160
  43.7 14.1 %all_gather.75 = bf16[512,384]{1,0:T(8,128)(2,1)S(1)} all-gather(bf16[128,384]{1,0:T(8,128)(2,1)} %param.25), channel_id=1, replica_groups=mesh['rep'=4,'shard'=4,'ctx'=2] {'shard'}, dimensions={0}, use_global_device_ids=true | all-gather | bytes 491520 | tf_op jit(solution)/shard_map/all_gather | solution.py:156
  57.7 16.5 %all_gather.76 = bf16[512,384]{1,0:T(8,128)(2,1)S(1)} all-gather(bf16[128,384]{1,0:T(8,128)(2,1)} %param.26), channel_id=1, replica_groups=mesh['rep'=4,'shard'=4,'ctx'=2] {'shard'}, dimensions={0}, use_global_device_ids=true | all-gather | bytes 491520 | tf_op jit(solution)/shard_map/all_gather | solution.py:157
  74.3 13.3 %all_gather.72 = bf16[512,384]{1,0:T(8,128)(2,1)} all-gather(bf16[128,384]{1,0:T(8,128)(2,1)} %param.27), channel_id=1, replica_groups=mesh['rep'=4,'shard'=4,'ctx'=2] {'shard'}, dimensions={0}, use_global_device_ids=true | all-gather | bytes 491520 | tf_op jit(solution)/shard_map/all_gather | solution.py:158
  87.5 17.0 %all_gather.79 = bf16[384,512]{1,0:T(8,128)(2,1)} all-gather(bf16[96,512]{1,0:T(8,128)(2,1)} %param.28), channel_id=1, replica_groups=mesh['rep'=4,'shard'=4,'ctx'=2] {'shard'}, dimensions={0}, use_global_device_ids=true | all-gather | bytes 491520 | tf_op jit(solution)/shard_map/all_gather | solution.py:159
  104.5 15.2 %all_gather.83 = bf16[512,384]{1,0:T(8,128)(2,1)S(1)} all-gather(bf16[128,384]{1,0:T(8,128)(2,1)} %param.31), channel_id=1, replica_groups=mesh['rep'=4,'shard'=4,'ctx'=2] {'shard'}, dimensions={0}, use_global_device_ids=true | all-gather | bytes 491520 | tf_op jit(solution)/shard_map/all_gather | solution.py:162
  119.7 11.7 %all_gather.84 = bf16[512,384]{1,0:T(8,128)(2,1)S(1)} all-gather(bf16[128,384]{1,0:T(8,128)(2,1)} %param.32), channel_id=1, replica_groups=mesh['rep'=4,'shard'=4,'ctx'=2] {'shard'}, dimensions={0}, use_global_device_ids=true | all-gather | bytes 491520 | tf_op jit(solution)/shard_map/all_gather | solution.py:163
  132.4 5.5 all_gather.85
  138.8 13.4 %all_gather.80 = bf16[512,384]{1,0:T(8,128)(2,1)S(1)} all-gather(bf16[128,384]{1,0:T(8,128)(2,1)S(1)} %copy-done.45), channel_id=1, replica_groups=mesh['rep'=4,'shard'=4,'ctx'=2] {'shard'}, dimensions={0}, use_global_device_ids=true | all-gather | bytes 491520 | tf_op jit(solution)/shard_map/all_gather | solution.py:164
  153.0 5.2 all_gather.81
  160.6 7.6 all_gather.77
  170.3 7.6 all_gather.73
  179.3 9.0 %convert_reduce_fusion = s32[512,1024]{1,0:T(8,128)S(1)} fusion(s32[512,1024]{1,0:T(8,128)} %broadcast_subtract_fusion, s32[31]{0:T(128)S(1)} %slice.4), kind=kLoop, calls=%fused_computation.3 | loop fusion | flops 48234496 | bytes 4194428 | tf_op jit(solution)/shard_map/reduce_sum | solution.py:66
  188.3 11.1 %iota_compare_fusion = pred[32,512,1024]{2,1,0:T(8,128)(4,1)} fusion(s32[512,1024]{1,0:T(8,128)S(1)} %convert_reduce_fusion), kind=kLoop, calls=%fused_computation.2 | loop fusion | flops 16777216 | bytes 18874368 | tf_op jit(solution)/shard_map/eq | solution.py:72
  199.4 100.9 %select_reduce_fusion.1 = f32[6,512,1024]{2,1,0:T(8,128)} fusion(f32[32,6]{1,0:T(8,128)S(1)} %convert_element_type.293, pred[32,512,1024]{2,1,0:T(8,128)(4,1)} %iota_compare_fusion), kind=kLoop, calls=%fused_computation.1 | loop fusion | flops 198180864 | bytes 29360896 | tf_op jit(solution)/shard_map/reduce_sum | solution.py:73
  300.4 6.0 fusion.66
  306.4 2.9 exponential_reduce_fusion
  310.9 2.4 fusion.21
  318.1 9.3 %all-gather.3 = bf16[4,1,128]{2,1,0:T(2,128)(2,1)S(1)} all-gather(bf16[1,1,128]{2,1,0:T(2,128)(2,1)S(1)} %bitcast.229), channel_id=1, replica_groups=mesh['rep'=4,'shard'=4,'ctx'=2] {'shard'}, dimensions={0}, use_global_device_ids=true | all-gather | bytes 1280 | tf_op jit(solution)/shard_map/all_gather | solution.py:166
  328.5 11.5 %all_gather.86 = bf16[384,512]{1,0:T(8,128)(2,1)S(1)} all-gather(bf16[96,512]{1,0:T(8,128)(2,1)S(1)} %copy-done.46), channel_id=1, replica_groups=mesh['rep'=4,'shard'=4,'ctx'=2] {'shard'}, dimensions={0}, use_global_device_ids=true | all-gather | bytes 491520 | tf_op jit(solution)/shard_map/all_gather | solution.py:165
  341.0 3.4 fusion.69
  344.4 3.3 fusion.68
  347.7 5.9 multiply_convert_fusion.2
  359.5 4.0 multiply_reduce_fusion.1
  363.5 6.4 multiply_convert_fusion.1
  377.4 6.9 fusion.13
  391.1 9.5 %multiply_reduce_fusion = (f32[6,512]{1,0:T(8,128)S(1)}, f32[6,512,1024]{2,1,0:T(8,128)}) fusion(f32[6,512,1024]{2,1,0:T(8,128)} %copy-done.1, f32[6,512]{1,0:T(8,128)S(1)} %log_add_fusion.1, bf16[512,6,64]{0,2,1:T(8,128)(2,1)} %bitcast.200, bf16[1024,6,64]{0,2,1:T(8,128)(2,1)} %bitcast.183), kind=kOutput, calls=%fused_computation.5 | convolution fusion | flops 412087296 | bytes 26370048 | tf_op jit(solution)/shard_map/qhd,khd->hqk/dot_general | solution.py:84
  400.7 14.3 %fusion.65 = (f32[6,512,1024]{2,1,0:T(8,128)}, bf16[6,512,1024]{2,1,0:T(8,128)(2,1)S(1)}) fusion(f32[6,512,1024]{2,1,0:T(8,128)} %get-tuple-element.133, f32[6,512]{1,0:T(8,128)S(1)} %get-tuple-element.132, f32[6,512,1024]{2,1,0:T(8,128)} %copy-done.1, f32[6,512]{1,0:T(8,128)S(1)} %log_add_fusion.1), kind=kLoop, calls=%fused_computation.132 | loop fusion | flops 15728640 | bytes 44064768 | tf_op jit(solution)/shard_map/convert_element_type | solution.py:80
  415.0 2.7 copy-done.3
  425.6 4.9 convolution_convert_fusion.3
  430.5 3.0 convolution_convert_fusion.2
  433.6 3.0 convolution_convert_fusion.1
  438.5 2.9 convolution_convert_fusion
  441.7 61.0 %select_reduce_fusion = bf16[32,6]{1,0:T(8,128)(2,1)S(1)} fusion(f32[6,512,1024]{2,1,0:T(8,128)} %get-tuple-element.115, pred[32,512,1024]{2,1,0:T(8,128)(4,1)} %iota_compare_fusion), kind=kLoop, calls=%fused_computation | loop fusion | flops 201326400 | bytes 29360512 | tf_op jit(solution)/shard_map/reduce_sum | solution.py:80
  510.3 16.0 %reduce-scatter.28.cloned.1.call-done = bf16[128,384]{1,0:T(8,128)(2,1)} async-done(((bf16[512,384]{1,0:T(8,128)(2,1)}), bf16[128,384]{1,0:T(8,128)(2,1)}) %reduce-scatter.28.cloned.1.call-update) | async-done | bytes 98320 | tf_op jit(solution)/shard_map/reduce_scatter | solution.py:352
  529.8 17.7 %reduce-scatter.48.cloned.1.call-done = bf16[128,384]{1,0:T(8,128)(2,1)} async-done(((bf16[512,384]{1,0:T(8,128)(2,1)}), bf16[128,384]{1,0:T(8,128)(2,1)}) %reduce-scatter.48.cloned.1.call-update) | async-done | bytes 98320
  548.5 20.0 %reduce-scatter.46.cloned.1.call-done = bf16[128,384]{1,0:T(8,128)(2,1)} async-done(((bf16[512,384]{1,0:T(8,128)(2,1)}), bf16[128,384]{1,0:T(8,128)(2,1)}) %reduce-scatter.46.cloned.1.call-update) | async-done | bytes 98320
  569.6 18.3 %reduce-scatter.20.cloned.1.call-done = bf16[512,384]{0,1:T(8,128)(2,1)} async-done(((bf16[1024,384]{0,1:T(8,128)(2,1)}), bf16[512,384]{0,1:T(8,128)(2,1)}) %reduce-scatter.20.cloned.1.call-update) | async-done | bytes 393232 | tf_op jit(solution)/shard_map/reduce_scatter | solution.py:300
  594.9 16.6 %all-reduce.5 = (bf16[512]{0:T(512)(128)(2,1)S(1)}, bf16[32,6]{1,0:T(8,128)(2,1)S(1)}, bf16[512]{0:T(512)(128)(2,1)S(1)}, bf16[512]{0:T(512)(128)(2,1)S(1)}) all-reduce(bf16[512]{0:T(512)(128)(2,1)S(1)} %get-tuple-element.94, bf16[32,6]{1,0:T(8,128)(2,1)S(1)} %select_reduce_fusion, ...), channel_id=7, replica_groups=mesh['rep'=4,'shard'=4,'ctx'=2] {'shard'}, use_global_device_ids=true, to_apply=%region_20.21.clone | all-reduce | flops 1728 | bytes 6912
  611.7 5.8 reduce-scatter.40.cloned.1.call-done
  617.5 28.0 %reduce-scatter.42.cloned.1.call-done = bf16[128,1024]{1,0:T(8,128)(2,1)} async-done(((bf16[512,1024]{1,0:T(8,128)(2,1)}), bf16[128,1024]{1,0:T(8,128)(2,1)}) %reduce-scatter.42.cloned.1.call-update) | async-done | bytes 262160 | tf_op jit(solution)/shard_map/reduce_scatter | solution.py:388
  645.6 28.0 %reduce-scatter.44.cloned.1.call-done = bf16[256,512]{1,0:T(8,128)(2,1)} async-done(((bf16[1024,512]{1,0:T(8,128)(2,1)}), bf16[256,512]{1,0:T(8,128)(2,1)}) %reduce-scatter.44.cloned.1.call-update) | async-done | bytes 262160 | tf_op jit(solution)/shard_map/reduce_scatter | solution.py:391
  673.5 21.0 %reduce-scatter.32.cloned.1.call-done = bf16[128,384]{1,0:T(8,128)(2,1)} async-done(((bf16[512,384]{1,0:T(8,128)(2,1)}), bf16[128,384]{1,0:T(8,128)(2,1)}) %reduce-scatter.32.cloned.1.call-update) | async-done | bytes 98320 | tf_op jit(solution)/shard_map/reduce_scatter | solution.py:358
  694.5 21.6 %reduce-scatter.30.cloned.1.call-done = bf16[128,384]{1,0:T(8,128)(2,1)} async-done(((bf16[512,384]{1,0:T(8,128)(2,1)}), bf16[128,384]{1,0:T(8,128)(2,1)}) %reduce-scatter.30.cloned.1.call-update) | async-done | bytes 98320 | tf_op jit(solution)/shard_map/reduce_scatter | solution.py:355
  716.1 132.1 %all-reduce.7 = (f32[128]{0:T(128)}, f32[128,384]{1,0:T(8,128)}, f32[128,384]{1,0:T(8,128)}, f32[128,384]{1,0:T(8,128)}, f32[96,512]{1,0:T(8,128)}, /*index=5*/f...) all-reduce(f32[128]{0:T(128)S(1)} %dynamic-slice_convert_fusion.3, ...), channel_id=1, replica_groups=mesh['rep'=4,'shard'=4,'ctx'=2] {'rep','ctx'}, use_global_device_ids=true, to_apply=%region_21.22 | all-reduce | flops 786864 | bytes 4722048 | tf_op jit(solution)/shard_map/psum | solution.py:395
  (228 shorter events, 74.7 us)
Async XLA Ops:
  7.2 124.9 %copy-start = (bf16[1,256,512]{2,1,0:T(8,128)(2,1)S(1)}, bf16[1,256,512]{2,1,0:T(8,128)(2,1)}, u32[]{:S(2)}) copy-start(bf16[1,256,512]{2,1,0:T(8,128)(2,1)} %param.21) | copy-start | bytes 786436
  7.2 131.6 %copy-start.45 = (bf16[128,384]{1,0:T(8,128)(2,1)S(1)}, bf16[128,384]{1,0:T(8,128)(2,1)}, u32[]{:S(2)}) copy-start(bf16[128,384]{1,0:T(8,128)(2,1)} %param.33) | copy-start | bytes 294916
  7.2 151.1 %copy-start.42 = (bf16[1,512,512]{2,1,0:T(8,128)(2,1)S(1)}, bf16[1,512,512]{2,1,0:T(8,128)(2,1)}, u32[]{:S(2)}) copy-start(bf16[1,512,512]{2,1,0:T(8,128)(2,1)} %param.20) | copy-start | bytes 1572868
  7.2 333.7 %all-gather.10.cloned.1.call-start = ((), (), s32[]{:S(2)}) async-start(), calls=%async_computation.16 | async-start | bytes 1310720 | tf_op jit(solution)/shard_map/all_gather | solution.py:168
  8.0 336.4 %all-gather.8.cloned.1.call-start = ((), (), s32[]{:S(2)}) async-start(), calls=%async_computation.15 | async-start | bytes 1310720 | tf_op jit(solution)/shard_map/all_gather | solution.py:167
  8.7 339.0 %all-gather.12.cloned.1.call-start = ((), (), s32[]{:S(2)}) async-start(), calls=%async_computation.17 | async-start | bytes 1310720 | tf_op jit(solution)/shard_map/all_gather | solution.py:169
  9.4 411.6 %reduce-scatter.26.cloned.1.call-start = ((), (), s32[]{:S(2)}) async-start(), calls=%async_computation.21 | async-start | bytes 589824 | tf_op jit(solution)/shard_map/reduce_scatter | solution.py:309
  57.7 102.3 %copy-start.37 = (bf16[512,384]{1,0:T(8,128)(2,1)}, bf16[512,384]{1,0:T(8,128)(2,1)S(1)}, u32[]{:S(2)}) copy-start(bf16[512,384]{1,0:T(8,128)(2,1)S(1)} %all_gather.75) | copy-start | bytes 1179652
  74.2 86.3 %copy-start.39 = (bf16[512,384]{1,0:T(8,128)(2,1)}, bf16[512,384]{1,0:T(8,128)(2,1)S(1)}, u32[]{:S(2)}) copy-start(bf16[512,384]{1,0:T(8,128)(2,1)S(1)} %all_gather.76) | copy-start | bytes 1179652
  119.7 194.2 %copy-start.17 = (bf16[512,384]{1,0:T(8,128)(2,1)}, bf16[512,384]{1,0:T(8,128)(2,1)S(1)}, u32[]{:S(2)}) copy-start(bf16[512,384]{1,0:T(8,128)(2,1)S(1)} %all_gather.83) | copy-start | bytes 1179652
  158.4 158.1 %copy-start.14 = (bf16[512,384]{0,1:T(8,128)(2,1)}, bf16[512,384]{0,1:T(8,128)(2,1)S(1)}, u32[]{:S(2)}) copy-start(bf16[512,384]{0,1:T(8,128)(2,1)S(1)} %copy.111) | copy-start | bytes 1179652
  158.6 154.7 %copy-start.6 = (bf16[1,512,512]{1,2,0:T(8,128)(2,1)}, bf16[1,512,512]{1,2,0:T(8,128)(2,1)S(1)}, u32[]{:S(2)}) copy-start(bf16[1,512,512]{1,2,0:T(8,128)(2,1)S(1)} %copy.108) | copy-start | bytes 1572868
  168.5 131.9 %copy-start.8 = (bf16[1024,384]{0,1:T(8,128)(2,1)}, bf16[1024,384]{0,1:T(8,128)(2,1)S(1)}, u32[]{:S(2)}) copy-start(bf16[1024,384]{0,1:T(8,128)(2,1)S(1)} %copy.110) | copy-start | bytes 2359300
  179.3 129.9 %copy-start.10 = (bf16[1024,384]{0,1:T(8,128)(2,1)}, bf16[1024,384]{0,1:T(8,128)(2,1)S(1)}, u32[]{:S(2)}) copy-start(bf16[1024,384]{0,1:T(8,128)(2,1)S(1)} %copy.109) | copy-start | bytes 2359300
  199.4 101.0 %copy-start.32 = (bf16[512,384]{0,1:T(8,128)(2,1)S(1)}, bf16[512,384]{0,1:T(8,128)(2,1)}, u32[]{:S(2)}) copy-start(bf16[512,384]{0,1:T(8,128)(2,1)} %convolution_convert_fusion.21) | copy-start | bytes 1179652
  199.4 101.0 %copy-start.34 = (pred[512,1024]{1,0:T(8,128)(4,1)S(1)}, pred[512,1024]{1,0:T(8,128)(4,1)}, u32[]{:S(2)}) copy-start(pred[512,1024]{1,0:T(8,128)(4,1)} %broadcast_compare_fusion) | copy-start | bytes 1572868
  315.5 12.0 %copy-start.43 = (bf16[1,512,512]{2,1,0:T(8,128)(2,1)S(1)}, bf16[1,512,512]{2,1,0:T(8,128)(2,1)}, u32[]{:S(2)}) copy-start(bf16[1,512,512]{2,1,0:T(8,128)(2,1)} %param.39) | copy-start | bytes 1572868
  315.5 13.0 %copy-start.46 = (bf16[96,512]{1,0:T(8,128)(2,1)S(1)}, bf16[96,512]{1,0:T(8,128)(2,1)}, u32[]{:S(2)}) copy-start(bf16[96,512]{1,0:T(8,128)(2,1)} %param.34) | copy-start | bytes 294916
  318.1 29.6 %copy-start.16 = (bf16[6,64,512]{2,1,0:T(8,128)(2,1)}, bf16[6,64,512]{2,1,0:T(8,128)(2,1)S(1)}, u32[]{:S(2)}) copy-start(bf16[6,64,512]{2,1,0:T(8,128)(2,1)S(1)} %convolution_convert_fusion.18) | copy-start | bytes 1179652
  340.5 15.1 %copy-start.4 = (f32[512,512]{0,1:T(8,128)}, f32[512,512]{0,1:T(8,128)S(1)}, u32[]{:S(2)}) copy-start(f32[512,512]{0,1:T(8,128)S(1)} %get-tuple-element.127) | copy-start | bytes 3145732
  340.9 12.7 %copy-start.11 = (bf16[512,512]{0,1:T(8,128)(2,1)}, bf16[512,512]{0,1:T(8,128)(2,1)S(1)}, u32[]{:S(2)}) copy-start(bf16[512,512]{0,1:T(8,128)(2,1)S(1)} %multiply_convert_fusion.4) | copy-start | bytes 1572868
  347.7 6.9 copy-start.13
  363.5 59.8 %reduce-scatter.24.cloned.1.call-start = ((), (), s32[]{:S(2)}) async-start(), calls=%async_computation.20 | async-start | bytes 589824 | tf_op jit(solution)/shard_map/reduce_scatter | solution.py:306
  363.5 6.5 copy-start.29
  363.5 7.1 copy-start.18
  374.1 130.3 %reduce-scatter.22.cloned.1.call-start = ((), (), s32[]{:S(2)}) async-start(), calls=%async_computation.19 | async-start | bytes 1179648 | tf_op jit(solution)/shard_map/reduce_scatter | solution.py:303
  377.4 6.9 copy-start.31
  384.4 125.9 %reduce-scatter.38.cloned.1.call-start = ((), (), s32[]{:S(2)}) async-start(), calls=%async_computation.27 | async-start | bytes 491520 | tf_op jit(solution)/shard_map/reduce_scatter | solution.py:379
  386.6 123.7 %reduce-scatter.36.cloned.1.call-start = ((), (), s32[]{:S(2)}) async-start(), calls=%async_computation.26 | async-start | bytes 491520 | tf_op jit(solution)/shard_map/reduce_scatter | solution.py:370
  391.1 119.2 %reduce-scatter.34.cloned.1.call-start = ((), (), s32[]{:S(2)}) async-start(), calls=%async_computation.25 | async-start | bytes 491520 | tf_op jit(solution)/shard_map/reduce_scatter | solution.py:361
  400.6 125.6 %reduce-scatter.28.cloned.1.call-start = ((), (), s32[]{:S(2)}) async-start(), calls=%async_computation.22 | async-start | bytes 491520 | tf_op jit(solution)/shard_map/reduce_scatter | solution.py:352
  400.7 17.0 %copy-start.9 = (bf16[1024,384]{0,1:T(8,128)(2,1)S(1)}, bf16[1024,384]{0,1:T(8,128)(2,1)}, u32[]{:S(2)}) copy-start(bf16[1024,384]{0,1:T(8,128)(2,1)} %copy-done.8) | copy-start | bytes 2359300
  417.7 7.9 copy-start.33
  421.0 126.5 %reduce-scatter.48.cloned.1.call-start = ((), (), s32[]{:S(2)}) async-start(), calls=%async_computation.32 | async-start | bytes 491520
  423.2 7.3 copy-start.12
  423.2 145.3 %reduce-scatter.46.cloned.1.call-start = ((), (), s32[]{:S(2)}) async-start(), calls=%async_computation.31 | async-start | bytes 491520
  425.5 162.3 %reduce-scatter.20.cloned.1.call-start = ((), (), s32[]{:S(2)}) async-start(), calls=%async_computation.18 | async-start | bytes 1179648 | tf_op jit(solution)/shard_map/reduce_scatter | solution.py:300
  430.5 8.1 copy-start.44
  430.5 187.0 %reduce-scatter.40.cloned.1.call-start = ((), (), s32[]{:S(2)}) async-start(), calls=%async_computation.28 | async-start | bytes 1310720 | tf_op jit(solution)/shard_map/reduce_scatter | solution.py:385
  433.5 212.0 %reduce-scatter.42.cloned.1.call-start = ((), (), s32[]{:S(2)}) async-start(), calls=%async_computation.29 | async-start | bytes 1310720 | tf_op jit(solution)/shard_map/reduce_scatter | solution.py:388
  436.6 237.0 %reduce-scatter.44.cloned.1.call-start = ((), (), s32[]{:S(2)}) async-start(), calls=%async_computation.30 | async-start | bytes 1310720 | tf_op jit(solution)/shard_map/reduce_scatter | solution.py:391
  441.5 253.0 %reduce-scatter.32.cloned.1.call-start = ((), (), s32[]{:S(2)}) async-start(), calls=%async_computation.24 | async-start | bytes 491520 | tf_op jit(solution)/shard_map/reduce_scatter | solution.py:358
  441.7 61.1 %copy-start.5 = (f32[512,512]{0,1:T(8,128)S(1)}, f32[512,512]{0,1:T(8,128)}, u32[]{:S(2)}) copy-start(f32[512,512]{0,1:T(8,128)} %copy-done.4) | copy-start | bytes 3145732
  441.7 61.1 %copy-start.48 = (bf16[1024,512]{1,0:T(8,128)(2,1)S(1)}, bf16[1024,512]{1,0:T(8,128)(2,1)}, u32[]{:S(2)}) copy-start(bf16[1024,512]{1,0:T(8,128)(2,1)} %all-gather.12.cloned.1.call-done) | copy-start | bytes 3145732
  441.7 61.1 %copy-start.50 = (bf16[512,1024]{1,0:T(8,128)(2,1)S(1)}, bf16[512,1024]{1,0:T(8,128)(2,1)}, u32[]{:S(2)}) copy-start(bf16[512,1024]{1,0:T(8,128)(2,1)} %get-tuple-element.119) | copy-start | bytes 3145732
  502.8 23.5 %copy-start.22 = (bf16[512,384]{1,0:T(8,128)(2,1)S(1)}, bf16[512,384]{1,0:T(8,128)(2,1)}, u32[]{:S(2)}) copy-start(bf16[512,384]{1,0:T(8,128)(2,1)} %copy-done.21) | copy-start | bytes 1179652
  506.6 209.5 %reduce-scatter.30.cloned.1.call-start = ((), (), s32[]{:S(2)}) async-start(), calls=%async_computation.23 | async-start | bytes 491520 | tf_op jit(solution)/shard_map/reduce_scatter | solution.py:355
  527.5 64.1 %copy-start.38 = (bf16[512,384]{1,0:T(8,128)(2,1)S(1)}, bf16[512,384]{1,0:T(8,128)(2,1)}, u32[]{:S(2)}) copy-start(bf16[512,384]{1,0:T(8,128)(2,1)} %all_gather.72) | copy-start | bytes 1179652
  (24 other events, 69.1 us)
Sparse Core Ops, SparseCore 0:
  9.6 29.9 all-gather.9
  41.2 36.6 all-gather.7
  79.4 37.5 all-gather.11
  363.6 41.9 reduce-scatter.25
  407.7 13.1 reduce-scatter.23
  423.0 17.4 reduce-scatter.21
  442.8 19.3 reduce-scatter.37
  464.5 18.8 reduce-scatter.35
  485.8 18.8 reduce-scatter.33
  507.3 18.8 reduce-scatter.27
  528.6 18.8 reduce-scatter.47
  549.7 18.8 reduce-scatter.45
  570.9 16.9 reduce-scatter.19
  590.0 27.4 reduce-scatter.39
  619.8 25.7 reduce-scatter.41
  647.7 25.7 reduce-scatter.43
  676.3 18.1 reduce-scatter.31
  697.2 18.8 reduce-scatter.29
where the time goes:
time: 863 us; the launch traced here: 857 us
  blocking collectives  326 us (38%)
  other arithmetic  214 us (25%)
  waiting for transfers between devices  179 us (21%)
  matrix products  98.9 us (11%)
  local copies, waits for them, and re-layouts  21.5 us (2%)
  between operations  16.7 us (2%)
    psum x1, blocking collectives, local(): lax.psum((owned_grads[0], owned_grads[1], owned_grads[2], owned_grads[3],...  132 us
    reduce_sum x1, other arithmetic, bucket_bias(): return jnp.sum(jnp.where(chosen, table[:, :, None, None], 0.0), axis=0)  101 us
    reduce_sum x1, other arithmetic, bucket_grad(): jnp.sum(jnp.where(chosen, score_grad[None].astype(jnp.float32), 0.0), axi...  61 us
    unnamed x20, waiting for transfers between devices  40 us
    reduce_scatter x1, waiting for transfers between devices, local(): lax.psum_scatter(local_grads[13].astype(jnp.bfloat16), 'shard', scatter_d...  28 us
    reduce_scatter x1, waiting for transfers between devices, local(): lax.psum_scatter(local_grads[14].astype(jnp.bfloat16), 'shard', scatter_d...  28 us
    dot_general x11, matrix products, left_matrix_product(): lax.dot_general(left, right, (((0,), (0,)), ((), ())), preferred_element_...  23.6 us
    reduce_scatter x1, waiting for transfers between devices, local(): lax.psum_scatter(local_grads[2].astype(jnp.bfloat16), 'shard', scatter_di...  21.6 us
  transfers between devices with their start and end apart: 18, of which 9 were waited for; matrix products, arithmetic and copies ran while one was open for 36% of the time, Pallas kernels for 0%

commit v1 on v0

v1 whole, which is shorter than its diff:
```python
import functools

import jax
import jax.numpy as jnp
from jax import lax
from jax.experimental import pallas as pl
from jax.experimental.pallas import tpu as pltpu
from jax.sharding import PartitionSpec as P

HEADS = 6
DH = 64
NB = 32
BLK = 64
SEQ = 1024
LANES = 128
PAIRS = HEADS * DH // LANES

epsilon = 1e-06
masked_value = -1e30


def rms_norm(inputs, gain):
    return inputs * lax.rsqrt(jnp.mean(inputs * inputs, axis=-1, keepdims=True) + epsilon) * gain


def gated_gelu(gate, upper):
    return jax.nn.gelu(gate, approximate=True) * upper


def product(left, right):
    return jnp.dot(left, right, preferred_element_type=jnp.float32)


def left_matrix_product(left, right):
    return lax.dot_general(
        left, right, (((0,), (0,)), ((), ())), preferred_element_type=jnp.float32
    )


def right_product(left, right):
    return lax.dot_general(
        left, right, (((1,), (1,)), ((), ())), preferred_element_type=jnp.float32
    )


def bits_of(size):
    bits, bit = [], 1
    while bit < size:
        bits.append(bit)
        bit *= 2
    return bits


def swap(value, axis, size, bit):
    return lax.ppermute(value, axis, [(i, i ^ bit) for i in range(size)])


def my_bit(axis, bit):
    return (lax.axis_index(axis) // bit) % 2 == 1


def double(value, axis, size, bit, dim=0):
    other = swap(value, axis, size, bit)
    high = my_bit(axis, bit)
    low_part = jnp.where(high, other, value)
    high_part = jnp.where(high, value, other)
    return jnp.concatenate([low_part, high_part], axis=dim)


def halve(value, axis, size, bit, dim=0):
    half = value.shape[dim] // 2
    high = my_bit(axis, bit)
    low_part = lax.slice_in_dim(value, 0, half, axis=dim)
    high_part = lax.slice_in_dim(value, half, 2 * half, axis=dim)
    keep = jnp.where(high, high_part, low_part)
    give = jnp.where(high, low_part, high_part).astype(jnp.bfloat16)
    got = swap(give, axis, size, bit)
    return keep.astype(jnp.float32) + got.astype(jnp.float32)


def gather_axis(value, axis, size):
    for bit in bits_of(size):
        value = double(value, axis, size, bit)
    return value


def reduce_axis(value, axis, size):
    for bit in reversed(bits_of(size)):
        value = halve(value, axis, size, bit)
    return value


def gather_shards(pack, shards, splits):
    piece = pack
    for axis, size, bit in splits:
        half = piece.shape[0] // 2
        piece = jnp.where(my_bit(axis, bit), piece[half:], piece[:half])
    me = lax.axis_index("shard")
    parts = [piece] + [swap(piece, "shard", shards, s) for s in range(1, shards)]
    whole = jnp.zeros((shards,) + piece.shape, piece.dtype)
    for s in range(shards):
        whole = lax.dynamic_update_slice(whole, parts[s][None], (me ^ s, 0, 0))
    for axis, size, bit in reversed(splits):
        whole = double(whole, axis, size, bit, dim=1)
    return whole


def reduce_shards(pack, shards, first, ways):
    val = pack.astype(jnp.bfloat16)
    for axis, size, bit in first:
        val = halve(val, axis, size, bit, dim=1).astype(jnp.bfloat16)
    me = lax.axis_index("shard")
    count = val.shape[1] // len(ways)
    done = []
    for n, way in enumerate(ways):
        part = val[:, n * count : (n + 1) * count]
        for axis, size, bit in way:
            part = halve(part, axis, size, bit, dim=1).astype(jnp.bfloat16)
        total = lax.dynamic_index_in_dim(part, me, 0, keepdims=False).astype(jnp.float32)
        for s in range(1, shards):
            give = lax.dynamic_index_in_dim(part, me ^ s, 0, keepdims=False)
            total = total + swap(give, "shard", shards, s).astype(jnp.float32)
        out = total.astype(jnp.bfloat16)
        for axis, size, bit in reversed(way):
            out = double(out, axis, size, bit)
        done.append(out)
    out = jnp.concatenate(done, axis=0)
    for axis, size, bit in reversed(first):
        out = double(out, axis, size, bit)
    return out


def to_lanes(value):
    count = value.shape[-1] // LANES
    return jnp.concatenate(
        [value[..., i * LANES : (i + 1) * LANES] for i in range(count)], axis=-2
    )


def from_lanes(value, columns):
    count = columns // LANES
    rows = value.shape[-2] // count
    return jnp.concatenate(
        [value[..., i * rows : (i + 1) * rows, :] for i in range(count)], axis=-1
    )


def lane_half(shape):
    return lax.broadcasted_iota(jnp.int32, shape, 1) // DH


def only(value, half, h):
    return jnp.where(half == h, value, jnp.zeros_like(value))


def band_start(block):
    odd = lax.rem(block, 2)
    return odd, pl.multiple_of(SEQ - BLK * block + BLK * odd, LANES)


def self_forward_kernel(all_blk, my_blk, w_ref, q_ref, k_ref, v_ref, o_ref, p_ref, ks, vs, sc, band):
    rows = q_ref.shape[0]
    for b in range(SEQ // BLK):
        at = pl.ds(pl.multiple_of(all_blk[b] * BLK, BLK), BLK)
        ks[at, :] = k_ref[b * BLK : (b + 1) * BLK, :]
        vs[at, :] = v_ref[b * BLK : (b + 1) * BLK, :]
    half = lane_half((rows, LANES))
    outs = []
    for h in range(2):
        line = jnp.broadcast_to(w_ref[h], (BLK, 2 * SEQ))
        line = pltpu.roll(line, 0, 1, stride=1, stride_axis=0)
        band[0] = line
        band[1] = pltpu.roll(line, BLK, 1)
        sc[...] = right_product(only(q_ref[...], half, h), ks[...])

        def body(i, carry):
            at = pl.ds(pl.multiple_of(i * BLK, BLK), BLK)
            odd, start = band_start(my_blk[i])
            s = sc[at, :] + band[odd, :, pl.ds(start, SEQ)]
            e = jnp.exp(s - jnp.max(s, axis=-1, keepdims=True))
            r = 1.0 / jnp.sum(e, axis=-1, keepdims=True)
            p_ref[h, at, :] = (e * r).astype(jnp.bfloat16)
            return carry

        lax.fori_loop(0, rows // BLK, body, 0)
        outs.append(product(p_ref[h], vs[...]))
    o_ref[...] = jnp.where(half == 0, outs[0], outs[1]).astype(jnp.bfloat16)


def self_backward_kernel(
    all_blk, my_blk, q_ref, k_ref, v_ref, do_ref, p_ref, dq_ref, dk_ref, dv_ref, dt_ref, ks, vs, sc, dsc, dks, dvs, band
):
    rows = q_ref.shape[0]
    for b in range(SEQ // BLK):
        at = pl.ds(pl.multiple_of(all_blk[b] * BLK, BLK), BLK)
        ks[at, :] = k_ref[b * BLK : (b + 1) * BLK, :]
        vs[at, :] = v_ref[b * BLK : (b + 1) * BLK, :]
    half = lane_half((rows, LANES))
    khalf = lane_half((SEQ, LANES))
    dqs = []
    for h in range(2):
        sc[...] = right_product(only(do_ref[...], half, h), vs[...])
        band[...] = jnp.zeros_like(band)

        def body(i, carry):
            at = pl.ds(pl.multiple_of(i * BLK, BLK), BLK)
            odd, start = band_start(my_blk[i])
            p = p_ref[h, at, :].astype(jnp.float32)
            dp = sc[at, :]
            ds = (p * (dp - jnp.sum(p * dp, axis=-1, keepdims=True))).astype(jnp.bfloat16)
            dsc[at, :] = ds
            band[odd, :, pl.ds(start, SEQ)] += ds.astype(jnp.float32)
            return carry

        lax.fori_loop(0, rows // BLK, body, 0)
        ds = dsc[...]
        dqs.append(product(ds, ks[...]))
        dk = left_matrix_product(ds, q_ref[...])
        dv = left_matrix_product(p_ref[h], do_ref[...])
        if h == 0:
            dks[...] = dk
            dvs[...] = dv
        else:
            dks[...] = jnp.where(khalf == 0, dks[...], dk)
            dvs[...] = jnp.where(khalf == 0, dvs[...], dv)
        total = band[0] + pltpu.roll(band[1], 2 * SEQ - BLK, 1)
        count = BLK
        while count > 8:
            count //= 2
            total = total[:count] + pltpu.roll(total[count:], 2 * SEQ - count, 1)
        row = lax.broadcasted_iota(jnp.int32, total.shape, 0)
        for bit in (4, 2, 1):
            total = jnp.where((row // bit) % 2 == 1, pltpu.roll(total, 2 * SEQ - bit, 1), total)
        dt_ref[h] = jnp.sum(total, axis=0, keepdims=True)
    dq_ref[...] = jnp.where(half == 0, dqs[0], dqs[1]).astype(jnp.bfloat16)
    for b in range(SEQ // BLK):
        at = pl.ds(pl.multiple_of(all_blk[b] * BLK, BLK), BLK)
        dk_ref[b * BLK : (b + 1) * BLK, :] = dks[at, :].astype(dk_ref.dtype)
        dv_ref[b * BLK : (b + 1) * BLK, :] = dvs[at, :].astype(dv_ref.dtype)


def cross_forward_kernel(q_ref, k_ref, v_ref, o_ref, p_ref):
    half = lane_half(q_ref.shape)
    outs = []
    for h in range(2):
        s = right_product(only(q_ref[...], half, h), k_ref[...])
        e = jnp.exp(s - jnp.max(s, axis=-1, keepdims=True))
        p_ref[h] = (e * (1.0 / jnp.sum(e, axis=-1, keepdims=True))).astype(jnp.bfloat16)
        outs.append(product(p_ref[h], v_ref[...]))
    o_ref[...] = jnp.where(half == 0, outs[0], outs[1]).astype(jnp.bfloat16)


def cross_backward_kernel(q_ref, k_ref, v_ref, do_ref, p_ref, dq_ref, dk_ref, dv_ref):
    half = lane_half(q_ref.shape)
    khalf = lane_half(k_ref.shape)
    dqs, dks, dvs = [], [], []
    for h in range(2):
        dp = right_product(only(do_ref[...], half, h), v_ref[...])
        p = p_ref[h].astype(jnp.float32)
        ds = (p * (dp - jnp.sum(p * dp, axis=-1, keepdims=True))).astype(jnp.bfloat16)
        dqs.append(product(ds, k_ref[...]))
        dks.append(left_matrix_product(ds, q_ref[...]))
        dvs.append(left_matrix_product(p_ref[h], do_ref[...]))
    dq_ref[...] = jnp.where(half == 0, dqs[0], dqs[1]).astype(jnp.bfloat16)
    dk_ref[...] = jnp.where(khalf == 0, dks[0], dks[1]).astype(dk_ref.dtype)
    dv_ref[...] = jnp.where(khalf == 0, dvs[0], dvs[1]).astype(dv_ref.dtype)


def column(rows, shift=0):
    return pl.BlockSpec((rows, LANES), lambda j: (0, j + shift))


def per_pair(*tail):
    return pl.BlockSpec((2,) + tail, lambda j: (j,) + (0,) * len(tail))


def shaped(*shape, dtype=jnp.bfloat16):
    return jax.ShapeDtypeStruct(shape, dtype)


scalars = pl.BlockSpec(memory_space=pltpu.SMEM)
params = pltpu.CompilerParams(vmem_limit_bytes=48 * 1024 * 1024)


def cost(flops, transcendentals=0):
    return pl.CostEstimate(flops=flops, bytes_accessed=16 << 20, transcendentals=transcendentals)


def self_forward(all_blk, my_blk, lines, query, kv):
    rows = query.shape[0]
    return pl.pallas_call(
        self_forward_kernel,
        grid=(PAIRS,),
        in_specs=[scalars, scalars, per_pair(1, 2 * SEQ), column(rows), column(SEQ), column(SEQ, PAIRS)],
        out_specs=[column(rows), per_pair(rows, SEQ)],
        out_shape=[shaped(rows, HEADS * DH), shaped(HEADS, rows, SEQ)],
        scratch_shapes=[
            pltpu.VMEM((SEQ, LANES), jnp.bfloat16),
            pltpu.VMEM((SEQ, LANES), jnp.bfloat16),
            pltpu.VMEM((rows, SEQ), jnp.float32),
            pltpu.VMEM((2, BLK, 2 * SEQ), jnp.float32),
        ],
        compiler_params=params,
        cost_estimate=cost(8 * HEADS * rows * SEQ * DH, HEADS * rows * SEQ),
        name="self_forward",
    )(all_blk, my_blk, lines, query, kv, kv)


def self_backward(all_blk, my_blk, query, kv, dout, probs):
    rows = query.shape[0]
    return pl.pallas_call(
        self_backward_kernel,
        grid=(PAIRS,),
        in_specs=[scalars, scalars, column(rows), column(SEQ), column(SEQ, PAIRS), column(rows), per_pair(rows, SEQ)],
        out_specs=[column(rows), column(SEQ), column(SEQ), per_pair(1, 2 * SEQ)],
        out_shape=[
            shaped(rows, HEADS * DH),
            shaped(SEQ, HEADS * DH),
            shaped(SEQ, HEADS * DH),
            shaped(HEADS, 1, 2 * SEQ, dtype=jnp.float32),
        ],
        scratch_shapes=[
            pltpu.VMEM((SEQ, LANES), jnp.bfloat16),
            pltpu.VMEM((SEQ, LANES), jnp.bfloat16),
            pltpu.VMEM((rows, SEQ), jnp.float32),
            pltpu.VMEM((rows, SEQ), jnp.bfloat16),
            pltpu.VMEM((SEQ, LANES), jnp.float32),
            pltpu.VMEM((SEQ, LANES), jnp.float32),
            pltpu.VMEM((2, BLK, 2 * SEQ), jnp.float32),
        ],
        compiler_params=params,
        cost_estimate=cost(16 * HEADS * rows * SEQ * DH),
        name="self_backward",
    )(all_blk, my_blk, query, kv, kv, dout, probs)


def cross_forward(query, kv):
    rows, length = query.shape[0], kv.shape[0]
    return pl.pallas_call(
        cross_forward_kernel,
        grid=(PAIRS,),
        in_specs=[column(rows), column(length), column(length, PAIRS)],
        out_specs=[column(rows), per_pair(rows, length)],
        out_shape=[shaped(rows, HEADS * DH), shaped(HEADS, rows, length)],
        compiler_params=params,
        cost_estimate=cost(8 * HEADS * rows * length * DH, HEADS * rows * length),
        name="cross_forward",
    )(query, kv, kv)


def cross_backward(query, kv, dout, probs):
    rows, length = query.shape[0], kv.shape[0]
    return pl.pallas_call(
        cross_backward_kernel,
        grid=(PAIRS,),
        in_specs=[column(rows), column(length), column(length, PAIRS), column(rows), per_pair(rows, length)],
        out_specs=[column(rows), column(length), column(length)],
        out_shape=[shaped(rows, HEADS * DH), shaped(length, HEADS * DH), shaped(length, HEADS * DH)],
        compiler_params=params,
        cost_estimate=cost(16 * HEADS * rows * length * DH),
        name="cross_backward",
    )(query, kv, kv, dout, probs)


def local(
    sizes,
    tokens,
    encoded,
    positions,
    bucket_table,
    gain_self,
    w_query,
    w_key,
    w_value,
    w_out,
    bias_table,
    gain_cross,
    c_query,
    c_key,
    c_value,
    c_out,
    gain_ff,
    w_gate,
    w_up,
    w_down,
    cotangent,
):
    reps, shards, ctxs = sizes
    core = [("rep", reps, 1)]
    rest = [("rep", reps, b) for b in bits_of(reps)[1:]]
    across = [("ctx", ctxs, b) for b in bits_of(ctxs)]
    inner = HEADS * DH
    owned_levels = bias_table.shape[0]
    width = tokens.shape[2]

    table_row = jnp.pad(bias_table.reshape(1, -1), ((0, 0), (0, LANES - bias_table.size)))
    small = [g.reshape(-1, LANES) for g in (gain_self, gain_cross, gain_ff)]
    small_rows = small[0].shape[0]
    extra = jnp.pad(
        jnp.concatenate(small + [table_row], axis=0), ((0, 32 - 3 * small_rows - 1), (0, 0))
    )
    early = jnp.concatenate([to_lanes(w) for w in (w_query, w_key, w_value, c_key, c_value)] + [extra])
    early_full = gather_shards(early, shards, core)
    late_names = (w_out, c_query, c_out, w_gate, w_up, w_down)
    late = jnp.concatenate([to_lanes(w) for w in late_names])
    late_full = gather_shards(late, shards, core)

    def unpack(full, shapes):
        outs, at = [], 0
        for rows, columns in shapes:
            count = rows * columns // LANES
            piece = from_lanes(full[:, at : at + count], columns)
            outs.append(piece.reshape(-1, columns))
            at += count
        return outs, at

    (self_query, self_key, self_value, cross_key, cross_value), at = unpack(
        early_full, [w_query.shape] * 5
    )
    gains = [
        early_full[:, at + i * small_rows : at + (i + 1) * small_rows].reshape(-1).astype(jnp.float32)
        for i in range(3)
    ]
    gain_one, gain_two, gain_three = gains
    table_full = early_full[:, at + 3 * small_rows, : bias_table.size].reshape(NB, HEADS)

    inputs = tokens[0].astype(jnp.float32)
    encoder = encoded[0]
    my_blk = positions[0][::BLK] // BLK
    all_blk = gather_axis(my_blk, "ctx", ctxs)
    levels = jnp.arange(NB, dtype=jnp.int32)
    member = (bucket_table[:, None] == levels[None, :]).astype(jnp.float32)
    by_offset = jnp.dot(member, table_full.astype(jnp.float32), precision=lax.Precision.HIGHEST)
    backwards = by_offset.T[:, ::-1]
    lines = jnp.concatenate(
        [
            jnp.full((HEADS, 1), masked_value, jnp.float32),
            backwards,
            jnp.full((HEADS, SEQ - 1), masked_value, jnp.float32),
        ],
        axis=1,
    )[:, None, :]

    hidden_first_layer = rms_norm(inputs, gain_one).astype(jnp.bfloat16)
    self_kv_weight = jnp.concatenate([self_key, self_value], axis=1)
    cross_kv_weight = jnp.concatenate([cross_key, cross_value], axis=1)
    own_kv = product(hidden_first_layer, self_kv_weight).astype(jnp.bfloat16)
    kv = gather_axis(own_kv, "ctx", ctxs)
    query = product(hidden_first_layer, self_query).astype(jnp.bfloat16)
    own_enc_kv = product(encoder, cross_kv_weight).astype(jnp.bfloat16)
    enc_kv = gather_axis(own_enc_kv, "ctx", ctxs)

    attn_one, probs_one = self_forward(all_blk, my_blk, lines, query, kv)

    (self_out, cross_query, cross_out, feed_gate, feed_up, feed_down), unused = unpack(
        late_full, [w.shape for w in late_names]
    )
    after_one = inputs + product(attn_one, self_out)
    hidden_two = rms_norm(after_one, gain_two).astype(jnp.bfloat16)
    cross_q = product(hidden_two, cross_query).astype(jnp.bfloat16)
    attn_two, probs_two = cross_forward(cross_q, enc_kv)
    after_two = after_one + product(attn_two, cross_out)
    hidden_three = rms_norm(after_two, gain_three).astype(jnp.bfloat16)
    gate = product(hidden_three, feed_gate)
    upper = product(hidden_three, feed_up)
    mixed = gated_gelu(gate, upper).astype(jnp.bfloat16)
    decoder_output = (after_two + product(mixed, feed_down)).astype(jnp.bfloat16)

    grad_low = cotangent[0]
    grad_res = grad_low.astype(jnp.float32)
    down_grad = left_matrix_product(mixed, grad_low)
    mixed_grad = right_product(grad_low, feed_down)
    unused, gelu_pull = jax.vjp(gated_gelu, gate, upper)
    gate_grad, upper_grad = gelu_pull(mixed_grad)
    gate_grad = gate_grad.astype(jnp.bfloat16)
    upper_grad = upper_grad.astype(jnp.bfloat16)
    wgate_grad = left_matrix_product(hidden_three, gate_grad)
    wup_grad = left_matrix_product(hidden_three, upper_grad)

    def pack_grads(grads):
        return jnp.concatenate(
            [
                to_lanes(g.astype(jnp.bfloat16).reshape(shards, -1, g.shape[1]))
                for g in grads
            ],
            axis=1,
        )

    ways = [rest + across, across + rest]
    feed_sum = reduce_shards(pack_grads((wgate_grad, wup_grad, down_grad)), shards, core, ways)

    hidden_grad = right_product(gate_grad, feed_gate) + right_product(upper_grad, feed_up)
    unused, norm_pull = jax.vjp(rms_norm, after_two, gain_three)
    back_three, feed_gain_grad = norm_pull(hidden_grad)
    grad_two = grad_res + back_three
    cross_low = grad_two.astype(jnp.bfloat16)
    cross_output_grad = left_matrix_product(attn_two, cross_low)
    attn_two_grad = right_product(cross_low, cross_out).astype(jnp.bfloat16)
    cq_grad, enckey_term, encvalue_term = cross_backward(cross_q, enc_kv, attn_two_grad, probs_two)
    enc_sum = reduce_axis(jnp.concatenate([enckey_term, encvalue_term], axis=1), "ctx", ctxs)
    enc_low = enc_sum.astype(jnp.bfloat16)
    cquery_grad = left_matrix_product(hidden_two, cq_grad)
    hidden_grad = right_product(cq_grad, cross_query)
    unused, norm_pull = jax.vjp(rms_norm, after_one, gain_two)
    back_two, cross_gain_grad = norm_pull(hidden_grad)
    grad_one = grad_two + back_two
    self_low = grad_one.astype(jnp.bfloat16)
    sout_grad = left_matrix_product(attn_one, self_low)
    attn_one_grad = right_product(self_low, self_out).astype(jnp.bfloat16)
    query_grad, key_term, value_term, line_grad = self_backward(
        all_blk, my_blk, query, kv, attn_one_grad, probs_one
    )
    kv_sum = reduce_axis(jnp.concatenate([key_term, value_term], axis=1), "ctx", ctxs)
    kv_low = kv_sum.astype(jnp.bfloat16)

    encoder_grad = right_product(enc_low, cross_kv_weight)
    enc_weight_grad = left_matrix_product(encoder, enc_low)
    squery_grad = left_matrix_product(hidden_first_layer, query_grad)
    kv_weight_grad = left_matrix_product(hidden_first_layer, kv_low)
    hidden_grad = right_product(query_grad, self_query) + right_product(kv_low, self_kv_weight)
    unused, norm_pull = jax.vjp(rms_norm, inputs, gain_one)
    back_one, self_gain_grad = norm_pull(hidden_grad)
    input_grad = grad_one + back_one

    offset_grad = line_grad[:, 0, 1 : SEQ + 1][:, ::-1]
    table_grad = jnp.dot(offset_grad, member, precision=lax.Precision.HIGHEST).T
    small_grads = [
        g.reshape(shards, small_rows, LANES)
        for g in (self_gain_grad, cross_gain_grad, feed_gain_grad)
    ]
    table_rows = table_grad.reshape(shards, 1, -1)
    table_rows = jnp.pad(table_rows, ((0, 0), (0, 0), (0, LANES - table_rows.shape[2])))
    pad_rows = 8 * reps * ctxs
    small_pack = jnp.concatenate(small_grads + [table_rows], axis=1)
    small_pack = jnp.pad(small_pack, ((0, 0), (0, pad_rows - small_pack.shape[1]), (0, 0)))
    attn_pack = jnp.concatenate(
        [
            pack_grads((squery_grad, kv_weight_grad, sout_grad, cquery_grad, enc_weight_grad, cross_output_grad)),
            small_pack.astype(jnp.bfloat16),
        ],
        axis=1,
    )
    attn_sum = reduce_shards(attn_pack, shards, core, ways)

    def unpack_sum(total, shapes):
        outs, at = [], 0
        for rows, columns in shapes:
            count = rows * columns // LANES
            outs.append(from_lanes(total[at : at + count], columns).astype(jnp.float32))
            at += count
        return outs, at

    (g_gate, g_up, g_down), unused = unpack_sum(feed_sum, [w_gate.shape, w_up.shape, w_down.shape])
    own = width // shards
    (g_query, g_kv, g_out, g_cquery, g_enc, g_cout), at = unpack_sum(
        attn_sum,
        [w_query.shape, (own, 2 * inner), w_out.shape, c_query.shape, (own, 2 * inner), c_out.shape],
    )
    tail = attn_sum[at:].astype(jnp.float32)
    g_gains = [tail[i * small_rows : (i + 1) * small_rows].reshape(-1) for i in range(3)]
    g_table = tail[3 * small_rows, : bias_table.size].reshape(owned_levels, HEADS)
    return (
        decoder_output[None],
        input_grad[None],
        encoder_grad[None],
        g_gains[0],
        g_query,
        g_kv[:, :inner],
        g_kv[:, inner:],
        g_out,
        g_table,
        g_gains[1],
        g_cquery,
        g_enc[:, :inner],
        g_enc[:, inner:],
        g_cout,
        g_gains[2],
        g_gate,
        g_up,
        g_down,
    )


def solution(mesh):
    sizes = tuple(mesh.shape[name] for name in ("rep", "shard", "ctx"))
    return jax.shard_map(
        functools.partial(local, sizes),
        mesh=mesh,
        in_specs=(
            P(("rep", "shard"), "ctx", None),
            P(("rep", "shard"), "ctx", None),
            P(("rep", "shard"), "ctx"),
            P(),
            P("shard"),
            P("shard", None),
            P("shard", None),
            P("shard", None),
            P("shard", None),
            P("shard", None),
            P("shard"),
            P("shard", None),
            P("shard", None),
            P("shard", None),
            P("shard", None),
            P("shard"),
            P("shard", None),
            P("shard", None),
            P("shard", None),
            P(("rep", "shard"), "ctx", None),
        ),
        out_specs=(
            P(("rep", "shard"), "ctx", None),
            P(("rep", "shard"), "ctx", None),
            P(("rep", "shard"), "ctx", None),
            P("shard"),
            P("shard", None),
            P("shard", None),
            P("shard", None),
            P("shard", None),
            P("shard", None),
            P("shard"),
            P("shard", None),
            P("shard", None),
            P("shard", None),
            P("shard", None),
            P("shard"),
            P("shard", None),
            P("shard", None),
            P("shard", None),
        ),
        check_vma=False,
    )
```

time: 863 us -> 346 us (0.40)
  blocking collectives: 326 us -> 0 us
  other arithmetic: 214 us -> 26.3 us
  waiting for transfers between devices: 179 us -> 97.4 us
  starting transfers between devices: 1.32 us -> 74.1 us
  matrix products: 98.9 us -> 28.4 us
  Pallas kernels: 0 us -> 48.5 us
  local copies, waits for them, and re-layouts: 21.5 us -> 62.5 us
  between operations: 16.7 us -> 2.74 us
    all_gather x17 -> x0, blocking collectives: 177 us -> none  [the longest x1 17 us: local(): lax.all_gather(owned[4], 'shard', axis=0, tiled=True)]
    reduce_sum x6 -> x0, other arithmetic: 176 us -> none  [the longest x1 101 us: bucket_bias(): return jnp.sum(jnp.where(chosen, table[:, :, None, None], 0.0), axis=0)]
    reduce_scatter x13 -> x0, waiting for transfers between devices: 139 us -> none  [the longest x1 28 us: local(): lax.psum_scatter(local_grads[13].astype(jnp.bfloat16), 'shard', scatter_d...]
    psum x1 -> x0, blocking collectives: 132 us -> none  [local(): lax.psum((owned_grads[0], owned_grads[1], owned_grads[2], owned_grads[3],...]
    ppermute x0 -> x45, waiting for transfers between devices: none -> 97.4 us  [swap(): return lax.ppermute(value, axis, [(i, i ^ bit) for i in range(size)])]
    ppermute x0 -> x45, starting transfers between devices: none -> 74.1 us  [swap(): return lax.ppermute(value, axis, [(i, i ^ bit) for i in range(size)])]
    pallas_call x0 -> x4, Pallas kernels: none -> 48.5 us  [the longest x1 19.2 us: self_forward(): pl.pallas_call(self_forward_kernel, grid=(PAIRS,), in_specs=[scalars, sca...]
    dot_general x12 -> x2, matrix products: 42.1 us -> 0.71 us  [the longest x1 0.37 us: local(): table_grad = jnp.dot(offset_grad, member, precision=lax.Precision.HIGHEST).T]
  transfers between devices with their start and end apart: 18 -> 45, of which waited for: 9 -> 20; matrix products, arithmetic and copies ran while one was open for 36% -> 20% of each run, Pallas kernels for 0% -> 6%
where the time goes in v1:
time: 346 us; the launch traced here: 340 us
  waiting for transfers between devices  97.4 us (28%)
  starting transfers between devices  74.1 us (21%)
  local copies, waits for them, and re-layouts  62.5 us (18%)
  Pallas kernels  48.5 us (14%)
  matrix products  28.4 us (8%)
  other arithmetic  26.3 us (8%)
    ppermute x45, waiting for transfers between devices, swap(): return lax.ppermute(value, axis, [(i, i ^ bit) for i in range(size)])  97.4 us
    ppermute x45, starting transfers between devices, swap(): return lax.ppermute(value, axis, [(i, i ^ bit) for i in range(size)])  74.1 us
    unnamed x203, local copies, waits for them, and re-layouts  48.1 us
    pallas_call x1, Pallas kernels, self_forward(): pl.pallas_call(self_forward_kernel, grid=(PAIRS,), in_specs=[scalars, sca...  19.2 us
    pallas_call x1, Pallas kernels, self_backward(): pl.pallas_call(self_backward_kernel, grid=(PAIRS,), in_specs=[scalars, sc...  19 us
    dot_general x9, matrix products, left_matrix_product(): lax.dot_general(left, right, (((0,), (0,)), ((), ())), preferred_element_...  11.3 us
    dot_general x9, matrix products, right_product(): lax.dot_general(left, right, (((1,), (1,)), ((), ())), preferred_element_...  10.2 us
  transfers between devices with their start and end apart: 45, of which 20 were waited for; matrix products, arithmetic and copies ran while one was open for 20% of the time, Pallas kernels for 6%

profile of v1, /device:TPU:1, one launch (start us, length us, event | category | flops | bytes accessed | tf_op | source)
XLA Modules:
  0.0 339.9 jit_solution(767437356244988976)
XLA Ops:
  14.1 2.1 collective-permute-start.1
  16.2 2.3 collective-permute-start.2
  21.3 1.6 broadcast_in_dim.75
  25.9 3.3 collective-permute-start.7
  31.5 3.5 %collective-permute-done.3 = bf16[976,128]{1,0:T(8,128)(2,1)} collective-permute-done((bf16[976,128]{1,0:T(8,128)(2,1)}, bf16[976,128]{1,0:T(8,128)(2,1)}, u32[]{:S(2)}, u32[]{:S(2)}) %collective-permute-start.3) | collective-permute-done | bytes 249888 | tf_op jit(solution)/shard_map/ppermute | solution.py:55
  36.0 4.2 %collective-permute-start.4 = (bf16[4,976,128]{2,1,0:T(8,128)(2,1)S(1)}, bf16[4,976,128]{2,1,0:T(8,128)(2,1)S(1)}, u32[]{:S(2)}, u32[]{:S(2)}) collective-permute-start(bf16[4,976,128]{2,1,0:T(8,128)(2,1)S(1)} %bitcast_dynamic-update-slice_fusion.4), channel_id=1, source_target_pairs={{0,8},{8,0},{16,24},{24,16},{1,9},{9,1},{17,25},{25,17},{2,10},{10... | collective-permute-start | bytes 2998280 | tf_op jit(solution)/shard_map/ppermute | solution.py:55
  40.2 10.0 %collective-permute-done.6 = bf16[2112,128]{1,0:T(8,128)(2,1)S(1)} collective-permute-done((bf16[2112,128]{1,0:T(8,128)(2,1)S(1)}, bf16[2112,128]{1,0:T(8,128)(2,1)S(1)}, u32[]{:S(2)}, u32[]{:S(2)}) %collective-permute-start.6) | collective-permute-done | bytes 540704 | tf_op jit(solution)/shard_map/ppermute | solution.py:55
  51.0 23.9 %collective-permute-done.7 = bf16[2112,128]{1,0:T(8,128)(2,1)S(1)} collective-permute-done((bf16[2112,128]{1,0:T(8,128)(2,1)S(1)}, bf16[2112,128]{1,0:T(8,128)(2,1)S(1)}, u32[]{:S(2)}, u32[]{:S(2)}) %collective-permute-start.7) | collective-permute-done | bytes 540704 | tf_op jit(solution)/shard_map/ppermute | solution.py:55
  76.6 3.2 collective-permute-start.9
  86.1 22.9 %collective-permute-done.10 = bf16[256,768]{1,0:T(8,128)(2,1)} collective-permute-done((bf16[256,768]{1,0:T(8,128)(2,1)S(1)}, bf16[256,768]{1,0:T(8,128)(2,1)}, u32[]{:S(2)}, u32[]{:S(2)}) %collective-permute-start.10) | collective-permute-done | bytes 393248 | tf_op jit(solution)/shard_map/ppermute | solution.py:55
  111.5 19.2 %self_forward.1 = (bf16[512,384]{1,0:T(8,128)(2,1)S(1)}, bf16[6,512,1024]{2,1,0:T(8,128)(2,1)}) custom-call(s32[16]{0:T(128)S(1)} %pad_add_fusion.all_blk, s32[8]{0:T(128)S(1)} %and_select_fusion.my_blk, f32[6,1,2048]{2,1,0:T(1,128)S(1)} %broadcast_in_dim.74.w_ref, bf16[512,384]{1,0:T(8,128)(2,1)S(1)} %convolution_convert_fusion.14.q_ref, ...), custom_call_target="tpu_custom_call" | custom-call | flops 1610612736 | bytes 16777216 | tf_op jit(solution)/shard_map/self_forward/pallas_call | solution.py:291
  130.7 2.5 broadcast_select_fusion
  135.4 4.1 %cross_forward.1 = (bf16[512,384]{1,0:T(8,128)(2,1)S(1)}, bf16[6,512,512]{2,1,0:T(8,128)(2,1)S(1)}) custom-call(bf16[512,384]{1,0:T(8,128)(2,1)S(1)} %convolution_convert_fusion.13.q_ref, bf16[512,768]{1,0:T(8,128)(2,1)S(1)} %pad_maximum_fusion.4.k_ref.v_ref, bf16[512,768]{1,0:T(8,128)(2,1)S(1)} %pad_maximum_fusion.4.k_ref.v_ref), custom_call_target="tpu_custom_call" | custom-call | flops 805306368 | bytes 16777216 | tf_op jit(solution)/shard_map/cross_forward/pallas_call | solution.py:339
  142.7 3.2 fusion.7
  149.0 6.2 %cross_backward.1 = (bf16[512,384]{1,0:T(8,128)(2,1)S(1)}, bf16[512,384]{1,0:T(8,128)(2,1)S(1)}, bf16[512,384]{1,0:T(8,128)(2,1)S(1)}) custom-call(bf16[512,384]{1,0:T(8,128)(2,1)S(1)} %convolution_convert_fusion.13.q_ref, bf16[512,768]{1,0:T(8,128)(2,1)S(1)} %pad_maximum_fusion.4.k_ref.v_ref, bf16[512,768]{1,0:T(8,128)(2,1)S(1)} %pad_maximum_fusion.4.k_ref.v_ref, ...), custom_call_target="tpu_custom_call" | custom-call | flops 1610612736 | bytes 16777216 | tf_op jit(solution)/shard_map/cross_backward/pallas_call | solution.py:353
  159.5 1.8 convolution_convert_fusion.2
  161.3 1.7 convolution_convert_fusion
  163.0 1.5 fusion.15
  164.5 1.7 convolution_convert_fusion.1
  166.2 19.0 %self_backward.1 = (bf16[512,384]{1,0:T(8,128)(2,1)S(1)}, bf16[1024,384]{1,0:T(8,128)(2,1)S(1)}, bf16[1024,384]{1,0:T(8,128)(2,1)S(1)}, f32[6,1,2048]{2,1,0:T(1,128)S(1)}) custom-call(s32[16]{0:T(128)S(1)} %pad_add_fusion.all_blk, s32[8]{0:T(128)S(1)} %and_select_fusion.my_blk, bf16[512,384]{1,0:T(8,128)(2,1)S(1)} %convolution_convert_fusion.14.q_ref, ...), custom_call_target="tpu_custom_call" | custom-call | flops 3221225472 | bytes 16777216 | tf_op jit(solution)/shard_map/self_backward/pallas_call | solution.py:311
  201.4 1.7 broadcast_select_fusion.3
  203.4 1.6 constant_dynamic-update-slice_fusion.94
  205.3 2.1 copy.80
  208.9 4.7 %collective-permute-done.12 = bf16[256,768]{1,0:T(8,128)(2,1)} collective-permute-done((bf16[256,768]{1,0:T(8,128)(2,1)}, bf16[256,768]{1,0:T(8,128)(2,1)}, u32[]{:S(2)}, u32[]{:S(2)}) %collective-permute-start.12) | collective-permute-done | bytes 393248 | tf_op jit(solution)/shard_map/ppermute | solution.py:55
  214.8 2.4 convolution_bitcast_fusion
  218.5 1.5 add_convert_fusion.2
  220.7 1.6 convolution_convert_fusion.3
  240.4 2.0 add_convert_fusion.1
  245.2 2.3 collective-permute-start.13
  247.5 4.0 %collective-permute-done.30 = bf16[4,384,128]{2,1,0:T(8,128)(2,1)S(1)} collective-permute-done((bf16[4,384,128]{2,1,0:T(8,128)(2,1)S(1)}, bf16[4,384,128]{2,1,0:T(8,128)(2,1)S(1)}, u32[]{:S(2)}, u32[]{:S(2)}) %collective-permute-start.30) | collective-permute-done | bytes 393248 | tf_op jit(solution)/shard_map/ppermute | solution.py:55
  254.5 3.0 collective-permute-done.38
  257.6 2.1 collective-permute-start.41
  259.7 8.6 %collective-permute-start.40 = (bf16[192,128]{1,0:T(8,128)(2,1)S(1)}, bf16[192,128]{1,0:T(8,128)(2,1)S(1)}, u32[]{:S(2)}, u32[]{:S(2)}) collective-permute-start(bf16[192,128]{1,0:T(8,128)(2,1)S(1)} %get-tuple-element.219), channel_id=1, source_target_pairs={{0,4},{2,6},{4,0},{6,2},{1,5},{3,7},{5,1},{7,3},{8,12},{10,14},{12... | collective-permute-start | bytes 147464 | tf_op jit(solution)/shard_map/ppermute | solution.py:55
  268.5 2.1 collective-permute-start.34
  273.3 2.5 collective-permute-done.33
  275.8 1.7 collective-permute-start.35
  279.4 1.9 collective-permute-done.43
  282.6 7.5 %collective-permute-start.44 = (bf16[1536,128]{1,0:T(8,128)(2,1)S(1)}, bf16[1536,128]{1,0:T(8,128)(2,1)S(1)}, u32[]{:S(2)}, u32[]{:S(2)}) collective-permute-start(bf16[1536,128]{1,0:T(8,128)(2,1)S(1)} %pad_maximum_fusion.18), channel_id=1, source_target_pairs={{0,8},{8,0},{16,24},{24,16},{1,9},{9,1},{17,25},{25,17},{2,10},{10... | collective-permute-start | bytes 1179656 | tf_op jit(solution)/shard_map/ppermute | solution.py:55
  293.2 8.6 %collective-permute-done.14 = bf16[4,392,128]{2,1,0:T(8,128)(2,1)S(1)} collective-permute-done((bf16[4,392,128]{2,1,0:T(8,128)(2,1)S(1)}, bf16[4,392,128]{2,1,0:T(8,128)(2,1)S(1)}, u32[]{:S(2)}, u32[]{:S(2)}) %collective-permute-start.14) | collective-permute-done | bytes 401440 | tf_op jit(solution)/shard_map/ppermute | solution.py:55
  305.2 2.8 collective-permute-done.22
  308.1 1.7 collective-permute-start.25
  309.9 1.8 collective-permute-start.23
  311.8 1.7 collective-permute-start.18
  313.6 1.9 collective-permute-start.16
  317.0 1.6 collective-permute-done.17
  318.7 1.5 collective-permute-start.19
  323.8 1.8 collective-permute-done.20
  325.7 5.3 %collective-permute-start.28 = (bf16[1568,128]{1,0:T(8,128)(2,1)S(1)}, bf16[1568,128]{1,0:T(8,128)(2,1)S(1)}, u32[]{:S(2)}, u32[]{:S(2)}) collective-permute-start(bf16[1568,128]{1,0:T(8,128)(2,1)S(1)} %pad_maximum_fusion.9), channel_id=1, source_target_pairs={{0,8},{8,0},{16,24},{24,16},{1,9},{9,1},{17,25},{25,17},{2,10},{10... | collective-permute-start | bytes 1204232 | tf_op jit(solution)/shard_map/ppermute | solution.py:55
  (405 shorter events, 117.2 us)
Async XLA Ops:
  0.7 82.7 %copy-start = (bf16[1,256,512]{2,1,0:T(8,128)(2,1)S(1)}, bf16[1,256,512]{2,1,0:T(8,128)(2,1)}, u32[]{:S(2)}) copy-start(bf16[1,256,512]{2,1,0:T(8,128)(2,1)} %param.21) | copy-start | bytes 786436
  0.7 20.0 %copy-start.31 = (bf16[96,512]{1,0:T(8,128)(2,1)S(1)}, bf16[96,512]{1,0:T(8,128)(2,1)}, u32[]{:S(2)}) copy-start(bf16[96,512]{1,0:T(8,128)(2,1)} %param.28) | copy-start | bytes 294916
  0.7 20.0 %copy-start.33 = (bf16[128,384]{1,0:T(8,128)(2,1)S(1)}, bf16[128,384]{1,0:T(8,128)(2,1)}, u32[]{:S(2)}) copy-start(bf16[128,384]{1,0:T(8,128)(2,1)} %param.31) | copy-start | bytes 294916
  14.1 15.1 %collective-permute-start.1 = (bf16[976,128]{1,0:T(8,128)(2,1)}, bf16[976,128]{1,0:T(8,128)(2,1)}, u32[]{:S(2)}, u32[]{:S(2)}) collective-permute-start(bf16[976,128]{1,0:T(8,128)(2,1)} %get-tuple-element.103), channel_id=1, source_target_pairs={{0,2},{2,0},{4,6},{6,4},{1,3},{3,1},{5,7},{7,5},{8,10},{10,8},{12,... | collective-permute-start | bytes 749576 | tf_op jit(solution)/shard_map/ppermute | solution.py:55
  16.2 14.3 %collective-permute-start.2 = (bf16[976,128]{1,0:T(8,128)(2,1)}, bf16[976,128]{1,0:T(8,128)(2,1)}, u32[]{:S(2)}, u32[]{:S(2)}) collective-permute-start(bf16[976,128]{1,0:T(8,128)(2,1)} %get-tuple-element.103), channel_id=1, source_target_pairs={{0,4},{2,6},{4,0},{6,2},{1,5},{3,7},{5,1},{7,3},{8,12},{10,14},{12... | collective-permute-start | bytes 749576 | tf_op jit(solution)/shard_map/ppermute | solution.py:55
  18.5 16.4 %collective-permute-start.3 = (bf16[976,128]{1,0:T(8,128)(2,1)}, bf16[976,128]{1,0:T(8,128)(2,1)}, u32[]{:S(2)}, u32[]{:S(2)}) collective-permute-start(bf16[976,128]{1,0:T(8,128)(2,1)} %get-tuple-element.103), channel_id=1, source_target_pairs={{0,6},{2,4},{4,2},{6,0},{1,7},{3,5},{5,3},{7,1},{8,14},{10,12},{12... | collective-permute-start | bytes 749576 | tf_op jit(solution)/shard_map/ppermute | solution.py:55
  19.3 6.6 %collective-permute-start = (s32[8]{0:T(128)S(1)}, s32[8]{0:T(128)S(1)}, u32[]{:S(2)}, u32[]{:S(2)}) collective-permute-start(s32[8]{0:T(128)S(1)} %and_select_fusion.my_blk), channel_id=1, source_target_pairs={{0,1},{1,0},{2,3},{3,2},{4,5},{5,4},{6,7},{7,6},{8,9},{9,8},{10,11... | collective-permute-start | bytes 104 | tf_op jit(solution)/shard_map/ppermute | solution.py:55
  23.9 26.3 %collective-permute-start.6 = (bf16[2112,128]{1,0:T(8,128)(2,1)S(1)}, bf16[2112,128]{1,0:T(8,128)(2,1)S(1)}, u32[]{:S(2)}, u32[]{:S(2)}) collective-permute-start(bf16[2112,128]{1,0:T(8,128)(2,1)S(1)} %get-tuple-element.101), channel_id=1, source_target_pairs={{0,2},{2,0},{4,6},{6,4},{1,3},{3,1},{5,7},{7,5},{8,10},{10,8},{12,... | collective-permute-start | bytes 1622024 | tf_op jit(solution)/shard_map/ppermute | solution.py:55
  25.9 49.1 %collective-permute-start.7 = (bf16[2112,128]{1,0:T(8,128)(2,1)S(1)}, bf16[2112,128]{1,0:T(8,128)(2,1)S(1)}, u32[]{:S(2)}, u32[]{:S(2)}) collective-permute-start(bf16[2112,128]{1,0:T(8,128)(2,1)S(1)} %get-tuple-element.101), channel_id=1, source_target_pairs={{0,4},{2,6},{4,0},{6,2},{1,5},{3,7},{5,1},{7,3},{8,12},{10,14},{12... | collective-permute-start | bytes 1622024 | tf_op jit(solution)/shard_map/ppermute | solution.py:55
  29.2 46.5 %collective-permute-start.8 = (bf16[2112,128]{1,0:T(8,128)(2,1)S(1)}, bf16[2112,128]{1,0:T(8,128)(2,1)S(1)}, u32[]{:S(2)}, u32[]{:S(2)}) collective-permute-start(bf16[2112,128]{1,0:T(8,128)(2,1)S(1)} %get-tuple-element.101), channel_id=1, source_target_pairs={{0,6},{2,4},{4,2},{6,0},{1,7},{3,5},{5,3},{7,1},{8,14},{10,12},{12... | collective-permute-start | bytes 1622024 | tf_op jit(solution)/shard_map/ppermute | solution.py:55
  36.0 43.9 %collective-permute-start.4 = (bf16[4,976,128]{2,1,0:T(8,128)(2,1)S(1)}, bf16[4,976,128]{2,1,0:T(8,128)(2,1)S(1)}, u32[]{:S(2)}, u32[]{:S(2)}) collective-permute-start(bf16[4,976,128]{2,1,0:T(8,128)(2,1)S(1)} %bitcast_dynamic-update-slice_fusion.4), channel_id=1, source_target_pairs={{0,8},{8,0},{16,24},{24,16},{1,9},{9,1},{17,25},{25,17},{2,10},{10... | collective-permute-start | bytes 2998280 | tf_op jit(solution)/shard_map/ppermute | solution.py:55
  76.6 54.0 %collective-permute-start.9 = (bf16[4,2112,128]{2,1,0:T(8,128)(2,1)}, bf16[4,2112,128]{2,1,0:T(8,128)(2,1)}, u32[]{:S(2)}, u32[]{:S(2)}) collective-permute-start(bf16[4,2112,128]{2,1,0:T(8,128)(2,1)} %bitcast_dynamic-update-slice_fusion), channel_id=1, source_target_pairs={{0,8},{8,0},{16,24},{24,16},{1,9},{9,1},{17,25},{25,17},{2,10},{10... | collective-permute-start | bytes 6488072 | tf_op jit(solution)/shard_map/ppermute | solution.py:55
  81.3 28.8 %collective-permute-start.5 = (bf16[512,768]{1,0:T(8,128)(2,1)S(1)}, bf16[512,768]{1,0:T(8,128)(2,1)}, u32[]{:S(2)}, u32[]{:S(2)}) collective-permute-start(bf16[512,768]{1,0:T(8,128)(2,1)S(1)} %convolution_convert_fusion.5), channel_id=1, source_target_pairs={{0,1},{1,0},{2,3},{3,2},{4,5},{5,4},{6,7},{7,6},{8,9},{9,8},{10,11... | collective-permute-start | bytes 2359304 | tf_op jit(solution)/shard_map/ppermute | solution.py:55
  83.7 25.2 %collective-permute-start.10 = (bf16[256,768]{1,0:T(8,128)(2,1)S(1)}, bf16[256,768]{1,0:T(8,128)(2,1)}, u32[]{:S(2)}, u32[]{:S(2)}) collective-permute-start(bf16[256,768]{1,0:T(8,128)(2,1)S(1)} %fusion.16), channel_id=1, source_target_pairs={{0,1},{1,0},{2,3},{3,2},{4,5},{5,4},{6,7},{7,6},{8,9},{9,8},{10,11... | collective-permute-start | bytes 1179656 | tf_op jit(solution)/shard_map/ppermute | solution.py:55
  186.6 31.9 %collective-permute-start.11 = (bf16[512,768]{1,0:T(8,128)(2,1)}, bf16[512,768]{1,0:T(8,128)(2,1)}, u32[]{:S(2)}, u32[]{:S(2)}) collective-permute-start(bf16[512,768]{1,0:T(8,128)(2,1)} %broadcast_select_fusion.6), channel_id=1, source_target_pairs={{0,1},{1,0},{2,3},{3,2},{4,5},{5,4},{6,7},{7,6},{8,9},{9,8},{10,11... | collective-permute-start | bytes 2359304 | tf_op jit(solution)/shard_map/ppermute | solution.py:55
  188.7 24.9 %collective-permute-start.12 = (bf16[256,768]{1,0:T(8,128)(2,1)}, bf16[256,768]{1,0:T(8,128)(2,1)}, u32[]{:S(2)}, u32[]{:S(2)}) collective-permute-start(bf16[256,768]{1,0:T(8,128)(2,1)} %broadcast_select_fusion.17), channel_id=1, source_target_pairs={{0,1},{1,0},{2,3},{3,2},{4,5},{5,4},{6,7},{7,6},{8,9},{9,8},{10,11... | collective-permute-start | bytes 1179656 | tf_op jit(solution)/shard_map/ppermute | solution.py:55
  207.6 32.8 %collective-permute-start.29 = (bf16[4,1536,128]{2,1,0:T(8,128)(2,1)}, bf16[4,1536,128]{2,1,0:T(8,128)(2,1)}, u32[]{:S(2)}, u32[]{:S(2)}) collective-permute-start(bf16[4,1536,128]{2,1,0:T(8,128)(2,1)} %broadcast_select_fusion.3), channel_id=1, source_target_pairs={{0,8},{8,0},{16,24},{24,16},{1,9},{9,1},{17,25},{25,17},{2,10},{10... | collective-permute-start | bytes 4718600 | tf_op jit(solution)/shard_map/ppermute | solution.py:55
  242.6 9.0 %collective-permute-start.30 = (bf16[4,384,128]{2,1,0:T(8,128)(2,1)S(1)}, bf16[4,384,128]{2,1,0:T(8,128)(2,1)S(1)}, u32[]{:S(2)}, u32[]{:S(2)}) collective-permute-start(bf16[4,384,128]{2,1,0:T(8,128)(2,1)S(1)} %get-tuple-element.134), channel_id=1, source_target_pairs={{0,16},{8,24},{16,0},{24,8},{1,17},{9,25},{17,1},{25,9},{2,18},{10... | collective-permute-start | bytes 1179656 | tf_op jit(solution)/shard_map/ppermute | solution.py:55
  243.9 8.7 %collective-permute-start.37 = (bf16[4,384,128]{2,1,0:T(8,128)(2,1)S(1)}, bf16[4,384,128]{2,1,0:T(8,128)(2,1)S(1)}, u32[]{:S(2)}, u32[]{:S(2)}) collective-permute-start(bf16[4,384,128]{2,1,0:T(8,128)(2,1)S(1)} %get-tuple-element.135), channel_id=1, source_target_pairs={{0,1},{1,0},{2,3},{3,2},{4,5},{5,4},{6,7},{7,6},{8,9},{9,8},{10,11... | collective-permute-start | bytes 1179656 | tf_op jit(solution)/shard_map/ppermute | solution.py:55
  245.2 44.9 %collective-permute-start.13 = (bf16[4,1568,128]{2,1,0:T(8,128)(2,1)S(1)}, bf16[4,1568,128]{2,1,0:T(8,128)(2,1)S(1)}, u32[]{:S(2)}, u32[]{:S(2)}) collective-permute-start(bf16[4,1568,128]{2,1,0:T(8,128)(2,1)S(1)} %broadcast_select_fusion.2), channel_id=1, source_target_pairs={{0,8},{8,0},{16,24},{24,16},{1,9},{9,1},{17,25},{25,17},{2,10},{10... | collective-permute-start | bytes 4816904 | tf_op jit(solution)/shard_map/ppermute | solution.py:55
  252.9 4.6 %collective-permute-start.38 = (bf16[4,192,128]{2,1,0:T(8,128)(2,1)S(1)}, bf16[4,192,128]{2,1,0:T(8,128)(2,1)S(1)}, u32[]{:S(2)}, u32[]{:S(2)}) collective-permute-start(bf16[4,192,128]{2,1,0:T(8,128)(2,1)S(1)} %broadcast_select_fusion.22), channel_id=1, source_target_pairs={{0,16},{8,24},{16,0},{24,8},{1,17},{9,25},{17,1},{25,9},{2,18},{10... | collective-permute-start | bytes 589832 | tf_op jit(solution)/shard_map/ppermute | solution.py:55
  253.3 15.1 %collective-permute-start.31 = (bf16[4,192,128]{2,1,0:T(8,128)(2,1)S(1)}, bf16[4,192,128]{2,1,0:T(8,128)(2,1)S(1)}, u32[]{:S(2)}, u32[]{:S(2)}) collective-permute-start(bf16[4,192,128]{2,1,0:T(8,128)(2,1)S(1)} %broadcast_select_fusion.23), channel_id=1, source_target_pairs={{0,1},{1,0},{2,3},{3,2},{4,5},{5,4},{6,7},{7,6},{8,9},{9,8},{10,11... | collective-permute-start | bytes 589832 | tf_op jit(solution)/shard_map/ppermute | solution.py:55
  257.6 13.0 %collective-permute-start.41 = (bf16[192,128]{1,0:T(8,128)(2,1)S(1)}, bf16[192,128]{1,0:T(8,128)(2,1)S(1)}, u32[]{:S(2)}, u32[]{:S(2)}) collective-permute-start(bf16[192,128]{1,0:T(8,128)(2,1)S(1)} %get-tuple-element.218), channel_id=1, source_target_pairs={{0,6},{2,4},{4,2},{6,0},{1,7},{3,5},{5,3},{7,1},{8,14},{10,12},{12... | collective-permute-start | bytes 147464 | tf_op jit(solution)/shard_map/ppermute | solution.py:55
  259.7 11.6 %collective-permute-start.40 = (bf16[192,128]{1,0:T(8,128)(2,1)S(1)}, bf16[192,128]{1,0:T(8,128)(2,1)S(1)}, u32[]{:S(2)}, u32[]{:S(2)}) collective-permute-start(bf16[192,128]{1,0:T(8,128)(2,1)S(1)} %get-tuple-element.219), channel_id=1, source_target_pairs={{0,4},{2,6},{4,0},{6,2},{1,5},{3,7},{5,1},{7,3},{8,12},{10,14},{12... | collective-permute-start | bytes 147464 | tf_op jit(solution)/shard_map/ppermute | solution.py:55
  268.3 3.9 %collective-permute-start.39 = (bf16[192,128]{1,0:T(8,128)(2,1)S(1)}, bf16[192,128]{1,0:T(8,128)(2,1)S(1)}, u32[]{:S(2)}, u32[]{:S(2)}) collective-permute-start(bf16[192,128]{1,0:T(8,128)(2,1)S(1)} %get-tuple-element.217), channel_id=1, source_target_pairs={{0,2},{2,0},{4,6},{6,4},{1,3},{3,1},{5,7},{7,5},{8,10},{10,8},{12,... | collective-permute-start | bytes 147464 | tf_op jit(solution)/shard_map/ppermute | solution.py:55
  268.5 4.8 %collective-permute-start.34 = (bf16[192,128]{1,0:T(8,128)(2,1)S(1)}, bf16[192,128]{1,0:T(8,128)(2,1)S(1)}, u32[]{:S(2)}, u32[]{:S(2)}) collective-permute-start(bf16[192,128]{1,0:T(8,128)(2,1)S(1)} %get-tuple-element.213), channel_id=1, source_target_pairs={{0,6},{2,4},{4,2},{6,0},{1,7},{3,5},{5,3},{7,1},{8,14},{10,12},{12... | collective-permute-start | bytes 147464 | tf_op jit(solution)/shard_map/ppermute | solution.py:55
  270.6 5.2 %collective-permute-start.33 = (bf16[192,128]{1,0:T(8,128)(2,1)S(1)}, bf16[192,128]{1,0:T(8,128)(2,1)S(1)}, u32[]{:S(2)}, u32[]{:S(2)}) collective-permute-start(bf16[192,128]{1,0:T(8,128)(2,1)S(1)} %get-tuple-element.214), channel_id=1, source_target_pairs={{0,4},{2,6},{4,0},{6,2},{1,5},{3,7},{5,1},{7,3},{8,12},{10,14},{12... | collective-permute-start | bytes 147464 | tf_op jit(solution)/shard_map/ppermute | solution.py:55
  271.3 4.5 %collective-permute-start.32 = (bf16[192,128]{1,0:T(8,128)(2,1)S(1)}, bf16[192,128]{1,0:T(8,128)(2,1)S(1)}, u32[]{:S(2)}, u32[]{:S(2)}) collective-permute-start(bf16[192,128]{1,0:T(8,128)(2,1)S(1)} %get-tuple-element.212), channel_id=1, source_target_pairs={{0,2},{2,0},{4,6},{6,4},{1,3},{3,1},{5,7},{7,5},{8,10},{10,8},{12,... | collective-permute-start | bytes 147464 | tf_op jit(solution)/shard_map/ppermute | solution.py:55
  272.2 5.3 %collective-permute-start.42 = (bf16[192,128]{1,0:T(8,128)(2,1)S(1)}, bf16[192,128]{1,0:T(8,128)(2,1)S(1)}, u32[]{:S(2)}, u32[]{:S(2)}) collective-permute-start(bf16[192,128]{1,0:T(8,128)(2,1)S(1)} %fusion.57), channel_id=1, source_target_pairs={{0,16},{8,24},{16,0},{24,8},{1,17},{9,25},{17,1},{25,9},{2,18},{10... | collective-permute-start | bytes 147464 | tf_op jit(solution)/shard_map/ppermute | solution.py:55
  275.8 3.1 collective-permute-start.35
  277.5 3.8 %collective-permute-start.43 = (bf16[384,128]{1,0:T(8,128)(2,1)S(1)}, bf16[384,128]{1,0:T(8,128)(2,1)S(1)}, u32[]{:S(2)}, u32[]{:S(2)}) collective-permute-start(bf16[384,128]{1,0:T(8,128)(2,1)S(1)} %pad_maximum_fusion.24), channel_id=1, source_target_pairs={{0,1},{1,0},{2,3},{3,2},{4,5},{5,4},{6,7},{7,6},{8,9},{9,8},{10,11... | collective-permute-start | bytes 294920 | tf_op jit(solution)/shard_map/ppermute | solution.py:55
  279.0 3.5 %collective-permute-start.36 = (bf16[384,128]{1,0:T(8,128)(2,1)S(1)}, bf16[384,128]{1,0:T(8,128)(2,1)S(1)}, u32[]{:S(2)}, u32[]{:S(2)}) collective-permute-start(bf16[384,128]{1,0:T(8,128)(2,1)S(1)} %pad_maximum_fusion.23), channel_id=1, source_target_pairs={{0,16},{8,24},{16,0},{24,8},{1,17},{9,25},{17,1},{25,9},{2,18},{10... | collective-permute-start | bytes 294920 | tf_op jit(solution)/shard_map/ppermute | solution.py:55
  282.6 10.2 %collective-permute-start.44 = (bf16[1536,128]{1,0:T(8,128)(2,1)S(1)}, bf16[1536,128]{1,0:T(8,128)(2,1)S(1)}, u32[]{:S(2)}, u32[]{:S(2)}) collective-permute-start(bf16[1536,128]{1,0:T(8,128)(2,1)S(1)} %pad_maximum_fusion.18), channel_id=1, source_target_pairs={{0,8},{8,0},{16,24},{24,16},{1,9},{9,1},{17,25},{25,17},{2,10},{10... | collective-permute-start | bytes 1179656 | tf_op jit(solution)/shard_map/ppermute | solution.py:55
  290.9 11.0 %collective-permute-start.14 = (bf16[4,392,128]{2,1,0:T(8,128)(2,1)S(1)}, bf16[4,392,128]{2,1,0:T(8,128)(2,1)S(1)}, u32[]{:S(2)}, u32[]{:S(2)}) collective-permute-start(bf16[4,392,128]{2,1,0:T(8,128)(2,1)S(1)} %get-tuple-element.130), channel_id=1, source_target_pairs={{0,16},{8,24},{16,0},{24,8},{1,17},{9,25},{17,1},{25,9},{2,18},{10... | collective-permute-start | bytes 1204232 | tf_op jit(solution)/shard_map/ppermute | solution.py:55
  291.4 10.6 %collective-permute-start.21 = (bf16[4,392,128]{2,1,0:T(8,128)(2,1)S(1)}, bf16[4,392,128]{2,1,0:T(8,128)(2,1)S(1)}, u32[]{:S(2)}, u32[]{:S(2)}) collective-permute-start(bf16[4,392,128]{2,1,0:T(8,128)(2,1)S(1)} %get-tuple-element.131), channel_id=1, source_target_pairs={{0,1},{1,0},{2,3},{3,2},{4,5},{5,4},{6,7},{7,6},{8,9},{9,8},{10,11... | collective-permute-start | bytes 1204232 | tf_op jit(solution)/shard_map/ppermute | solution.py:55
  302.4 5.5 %collective-permute-start.22 = (bf16[4,196,128]{2,1,0:T(8,128)(2,1)S(1)}, bf16[4,196,128]{2,1,0:T(8,128)(2,1)S(1)}, u32[]{:S(2)}, u32[]{:S(2)}) collective-permute-start(bf16[4,196,128]{2,1,0:T(8,128)(2,1)S(1)} %broadcast_select_fusion.20), channel_id=1, source_target_pairs={{0,16},{8,24},{16,0},{24,8},{1,17},{9,25},{17,1},{25,9},{2,18},{10... | collective-permute-start | bytes 602120 | tf_op jit(solution)/shard_map/ppermute | solution.py:55
  303.8 7.9 %collective-permute-start.15 = (bf16[4,196,128]{2,1,0:T(8,128)(2,1)S(1)}, bf16[4,196,128]{2,1,0:T(8,128)(2,1)S(1)}, u32[]{:S(2)}, u32[]{:S(2)}) collective-permute-start(bf16[4,196,128]{2,1,0:T(8,128)(2,1)S(1)} %broadcast_select_fusion.21), channel_id=1, source_target_pairs={{0,1},{1,0},{2,3},{3,2},{4,5},{5,4},{6,7},{7,6},{8,9},{9,8},{10,11... | collective-permute-start | bytes 602120 | tf_op jit(solution)/shard_map/ppermute | solution.py:55
  308.1 5.5 %collective-permute-start.25 = (bf16[196,128]{1,0:T(8,128)(2,1)S(1)}, bf16[196,128]{1,0:T(8,128)(2,1)S(1)}, u32[]{:S(2)}, u32[]{:S(2)}) collective-permute-start(bf16[196,128]{1,0:T(8,128)(2,1)S(1)} %get-tuple-element.204), channel_id=1, source_target_pairs={{0,6},{2,4},{4,2},{6,0},{1,7},{3,5},{5,3},{7,1},{8,14},{10,12},{12... | collective-permute-start | bytes 150536 | tf_op jit(solution)/shard_map/ppermute | solution.py:55
  309.8 5.6 %collective-permute-start.24 = (bf16[196,128]{1,0:T(8,128)(2,1)S(1)}, bf16[196,128]{1,0:T(8,128)(2,1)S(1)}, u32[]{:S(2)}, u32[]{:S(2)}) collective-permute-start(bf16[196,128]{1,0:T(8,128)(2,1)S(1)} %get-tuple-element.205), channel_id=1, source_target_pairs={{0,4},{2,6},{4,0},{6,2},{1,5},{3,7},{5,1},{7,3},{8,12},{10,14},{12... | collective-permute-start | bytes 150536 | tf_op jit(solution)/shard_map/ppermute | solution.py:55
  309.9 5.5 %collective-permute-start.23 = (bf16[196,128]{1,0:T(8,128)(2,1)S(1)}, bf16[196,128]{1,0:T(8,128)(2,1)S(1)}, u32[]{:S(2)}, u32[]{:S(2)}) collective-permute-start(bf16[196,128]{1,0:T(8,128)(2,1)S(1)} %get-tuple-element.203), channel_id=1, source_target_pairs={{0,2},{2,0},{4,6},{6,4},{1,3},{3,1},{5,7},{7,5},{8,10},{10,8},{12,... | collective-permute-start | bytes 150536 | tf_op jit(solution)/shard_map/ppermute | solution.py:55
  311.8 5.1 %collective-permute-start.18 = (bf16[196,128]{1,0:T(8,128)(2,1)S(1)}, bf16[196,128]{1,0:T(8,128)(2,1)S(1)}, u32[]{:S(2)}, u32[]{:S(2)}) collective-permute-start(bf16[196,128]{1,0:T(8,128)(2,1)S(1)} %get-tuple-element.201), channel_id=1, source_target_pairs={{0,6},{2,4},{4,2},{6,0},{1,7},{3,5},{5,3},{7,1},{8,14},{10,12},{12... | collective-permute-start | bytes 150536 | tf_op jit(solution)/shard_map/ppermute | solution.py:55
  313.6 5.0 %collective-permute-start.17 = (bf16[196,128]{1,0:T(8,128)(2,1)S(1)}, bf16[196,128]{1,0:T(8,128)(2,1)S(1)}, u32[]{:S(2)}, u32[]{:S(2)}) collective-permute-start(bf16[196,128]{1,0:T(8,128)(2,1)S(1)} %get-tuple-element.202), channel_id=1, source_target_pairs={{0,4},{2,6},{4,0},{6,2},{1,5},{3,7},{5,1},{7,3},{8,12},{10,14},{12... | collective-permute-start | bytes 150536 | tf_op jit(solution)/shard_map/ppermute | solution.py:55
  313.6 5.0 %collective-permute-start.16 = (bf16[196,128]{1,0:T(8,128)(2,1)S(1)}, bf16[196,128]{1,0:T(8,128)(2,1)S(1)}, u32[]{:S(2)}, u32[]{:S(2)}) collective-permute-start(bf16[196,128]{1,0:T(8,128)(2,1)S(1)} %get-tuple-element.200), channel_id=1, source_target_pairs={{0,2},{2,0},{4,6},{6,4},{1,3},{3,1},{5,7},{7,5},{8,10},{10,8},{12,... | collective-permute-start | bytes 150536 | tf_op jit(solution)/shard_map/ppermute | solution.py:55
  315.5 4.6 %collective-permute-start.26 = (bf16[196,128]{1,0:T(8,128)(2,1)S(1)}, bf16[196,128]{1,0:T(8,128)(2,1)S(1)}, u32[]{:S(2)}, u32[]{:S(2)}) collective-permute-start(bf16[196,128]{1,0:T(8,128)(2,1)S(1)} %fusion.48), channel_id=1, source_target_pairs={{0,16},{8,24},{16,0},{24,8},{1,17},{9,25},{17,1},{25,9},{2,18},{10... | collective-permute-start | bytes 150536 | tf_op jit(solution)/shard_map/ppermute | solution.py:55
  318.7 3.0 collective-permute-start.19
  320.2 3.6 %collective-permute-start.27 = (bf16[392,128]{1,0:T(8,128)(2,1)S(1)}, bf16[392,128]{1,0:T(8,128)(2,1)S(1)}, u32[]{:S(2)}, u32[]{:S(2)}) collective-permute-start(bf16[392,128]{1,0:T(8,128)(2,1)S(1)} %pad_maximum_fusion.21), channel_id=1, source_target_pairs={{0,1},{1,0},{2,3},{3,2},{4,5},{5,4},{6,7},{7,6},{8,9},{9,8},{10,11... | collective-permute-start | bytes 301064 | tf_op jit(solution)/shard_map/ppermute | solution.py:55
  321.7 3.8 %collective-permute-start.20 = (bf16[392,128]{1,0:T(8,128)(2,1)S(1)}, bf16[392,128]{1,0:T(8,128)(2,1)S(1)}, u32[]{:S(2)}, u32[]{:S(2)}) collective-permute-start(bf16[392,128]{1,0:T(8,128)(2,1)S(1)} %pad_maximum_fusion.20), channel_id=1, source_target_pairs={{0,16},{8,24},{16,0},{24,8},{1,17},{9,25},{17,1},{25,9},{2,18},{10... | collective-permute-start | bytes 301064 | tf_op jit(solution)/shard_map/ppermute | solution.py:55
  325.7 7.8 %collective-permute-start.28 = (bf16[1568,128]{1,0:T(8,128)(2,1)S(1)}, bf16[1568,128]{1,0:T(8,128)(2,1)S(1)}, u32[]{:S(2)}, u32[]{:S(2)}) collective-permute-start(bf16[1568,128]{1,0:T(8,128)(2,1)S(1)} %pad_maximum_fusion.9), channel_id=1, source_target_pairs={{0,8},{8,0},{16,24},{24,16},{1,9},{9,1},{17,25},{25,17},{2,10},{10... | collective-permute-start | bytes 1204232 | tf_op jit(solution)/shard_map/ppermute | solution.py:55
  (35 other events, 139.1 us)

commit v2 on v1

--- a/solution.py
+++ b/solution.py
@@ -90,11 +90,13 @@
     return value
 
 
-def gather_shards(pack, shards, splits):
+def gather_shards(pack, shards, splits, after=None):
     piece = pack
     for axis, size, bit in splits:
         half = piece.shape[0] // 2
         piece = jnp.where(my_bit(axis, bit), piece[half:], piece[:half])
+    if after is not None:
+        piece, unused = lax.optimization_barrier((piece, after))
     me = lax.axis_index("shard")
     parts = [piece] + [swap(piece, "shard", shards, s) for s in range(1, shards)]
     whole = jnp.zeros((shards,) + piece.shape, piece.dtype)
@@ -102,32 +104,45 @@
         whole = lax.dynamic_update_slice(whole, parts[s][None], (me ^ s, 0, 0))
     for axis, size, bit in reversed(splits):
         whole = double(whole, axis, size, bit, dim=1)
-    return whole
-
-
-def reduce_shards(pack, shards, first, ways):
-    val = pack.astype(jnp.bfloat16)
-    for axis, size, bit in first:
-        val = halve(val, axis, size, bit, dim=1).astype(jnp.bfloat16)
-    me = lax.axis_index("shard")
-    count = val.shape[1] // len(ways)
-    done = []
-    for n, way in enumerate(ways):
-        part = val[:, n * count : (n + 1) * count]
-        for axis, size, bit in way:
-            part = halve(part, axis, size, bit, dim=1).astype(jnp.bfloat16)
-        total = lax.dynamic_index_in_dim(part, me, 0, keepdims=False).astype(jnp.float32)
-        for s in range(1, shards):
-            give = lax.dynamic_index_in_dim(part, me ^ s, 0, keepdims=False)
-            total = total + swap(give, "shard", shards, s).astype(jnp.float32)
-        out = total.astype(jnp.bfloat16)
-        for axis, size, bit in reversed(way):
+    return whole, parts[-1]
+
+
+class Reduction:
+    def __init__(self, pack, shards, first, ways):
+        self.val, self.shards, self.first, self.ways = pack, shards, first, ways
+
+    def first_stage(self):
+        val = self.val.astype(jnp.bfloat16)
+        for axis, size, bit in self.first:
+            val = halve(val, axis, size, bit, dim=1).astype(jnp.bfloat16)
+        count = val.shape[1] // len(self.ways)
+        self.parts = [val[:, n * count : (n + 1) * count] for n in range(len(self.ways))]
+        return val
+
+    def across_stage(self, steps):
+        for n, way in enumerate(self.ways):
+            for axis, size, bit in way[steps]:
+                self.parts[n] = halve(self.parts[n], axis, size, bit, dim=1).astype(jnp.bfloat16)
+        return self.parts[0]
+
+    def shard_stage(self):
+        me = lax.axis_index("shard")
+        for n, part in enumerate(self.parts):
+            total = lax.dynamic_index_in_dim(part, me, 0, keepdims=False).astype(jnp.float32)
+            for s in range(1, self.shards):
+                give = lax.dynamic_index_in_dim(part, me ^ s, 0, keepdims=False)
+                total = total + swap(give, "shard", self.shards, s).astype(jnp.float32)
+            self.parts[n] = total.astype(jnp.bfloat16)
+        return self.parts[0]
+
+    def back_stage(self):
+        for n, way in enumerate(self.ways):
+            for axis, size, bit in reversed(way):
+                self.parts[n] = double(self.parts[n], axis, size, bit)
+        out = jnp.concatenate(self.parts, axis=0)
+        for axis, size, bit in reversed(self.first):
             out = double(out, axis, size, bit)
-        done.append(out)
-    out = jnp.concatenate(done, axis=0)
-    for axis, size, bit in reversed(first):
-        out = double(out, axis, size, bit)
-    return out
+        return out
 
 
 def to_lanes(value):
@@ -187,9 +202,8 @@
     o_ref[...] = jnp.where(half == 0, outs[0], outs[1]).astype(jnp.bfloat16)
 
 
-def self_backward_kernel(
-    all_blk, my_blk, q_ref, k_ref, v_ref, do_ref, p_ref, dq_ref, dk_ref, dv_ref, dt_ref, ks, vs, sc, dsc, dks, dvs, band
-):
+def self_backward_kernel(ties, all_blk, my_blk, q_ref, k_ref, v_ref, do_ref, p_ref, *refs):
+    dq_ref, dk_ref, dv_ref, dt_ref, ks, vs, sc, dsc, dks, dvs, band = refs[ties:]
     rows = q_ref.shape[0]
     for b in range(SEQ // BLK):
         at = pl.ds(pl.multiple_of(all_blk[b] * BLK, BLK), BLK)
@@ -250,7 +264,7 @@
     o_ref[...] = jnp.where(half == 0, outs[0], outs[1]).astype(jnp.bfloat16)
 
 
-def cross_backward_kernel(q_ref, k_ref, v_ref, do_ref, p_ref, dq_ref, dk_ref, dv_ref):
+def cross_backward_kernel(q_ref, k_ref, v_ref, do_ref, p_ref, tie_ref, dq_ref, dk_ref, dv_ref):
     half = lane_half(q_ref.shape)
     khalf = lane_half(k_ref.shape)
     dqs, dks, dvs = [], [], []
@@ -279,6 +293,7 @@
 
 
 scalars = pl.BlockSpec(memory_space=pltpu.SMEM)
+anywhere = pl.BlockSpec(memory_space=pl.ANY)
 params = pltpu.CompilerParams(vmem_limit_bytes=48 * 1024 * 1024)
 
 
@@ -306,18 +321,20 @@
     )(all_blk, my_blk, lines, query, kv, kv)
 
 
-def self_backward(all_blk, my_blk, query, kv, dout, probs):
+def self_backward(pair, all_blk, my_blk, query, kv, dout, probs, ties):
     rows = query.shape[0]
+    specs = [column(rows, pair), column(SEQ, pair), column(SEQ, PAIRS + pair), column(rows, pair)]
+    probs_spec = pl.BlockSpec((2, rows, SEQ), lambda j: (j + pair, 0, 0))
     return pl.pallas_call(
-        self_backward_kernel,
-        grid=(PAIRS,),
-        in_specs=[scalars, scalars, column(rows), column(SEQ), column(SEQ, PAIRS), column(rows), per_pair(rows, SEQ)],
+        functools.partial(self_backward_kernel, len(ties)),
+        grid=(1,),
+        in_specs=[scalars, scalars] + specs + [probs_spec] + [anywhere] * len(ties),
         out_specs=[column(rows), column(SEQ), column(SEQ), per_pair(1, 2 * SEQ)],
         out_shape=[
-            shaped(rows, HEADS * DH),
-            shaped(SEQ, HEADS * DH),
-            shaped(SEQ, HEADS * DH),
-            shaped(HEADS, 1, 2 * SEQ, dtype=jnp.float32),
+            shaped(rows, LANES),
+            shaped(SEQ, LANES),
+            shaped(SEQ, LANES),
+            shaped(2, 1, 2 * SEQ, dtype=jnp.float32),
         ],
         scratch_shapes=[
             pltpu.VMEM((SEQ, LANES), jnp.bfloat16),
@@ -329,9 +346,9 @@
             pltpu.VMEM((2, BLK, 2 * SEQ), jnp.float32),
         ],
         compiler_params=params,
-        cost_estimate=cost(16 * HEADS * rows * SEQ * DH),
+        cost_estimate=cost(16 * 2 * rows * SEQ * DH),
         name="self_backward",
-    )(all_blk, my_blk, query, kv, kv, dout, probs)
+    )(all_blk, my_blk, query, kv, kv, dout, probs, *ties)
 
 
 def cross_forward(query, kv):
@@ -348,18 +365,18 @@
     )(query, kv, kv)
 
 
-def cross_backward(query, kv, dout, probs):
+def cross_backward(query, kv, dout, probs, tie):
     rows, length = query.shape[0], kv.shape[0]
     return pl.pallas_call(
         cross_backward_kernel,
         grid=(PAIRS,),
-        in_specs=[column(rows), column(length), column(length, PAIRS), column(rows), per_pair(rows, length)],
+        in_specs=[column(rows), column(length), column(length, PAIRS), column(rows), per_pair(rows, length), anywhere],
         out_specs=[column(rows), column(length), column(length)],
         out_shape=[shaped(rows, HEADS * DH), shaped(length, HEADS * DH), shaped(length, HEADS * DH)],
         compiler_params=params,
         cost_estimate=cost(16 * HEADS * rows * length * DH),
         name="cross_backward",
-    )(query, kv, kv, dout, probs)
+    )(query, kv, kv, dout, probs, tie)
 
 
 def local(
@@ -400,10 +417,10 @@
         jnp.concatenate(small + [table_row], axis=0), ((0, 32 - 3 * small_rows - 1), (0, 0))
     )
     early = jnp.concatenate([to_lanes(w) for w in (w_query, w_key, w_value, c_key, c_value)] + [extra])
-    early_full = gather_shards(early, shards, core)
+    early_full, early_part = gather_shards(early, shards, core + across[:1])
     late_names = (w_out, c_query, c_out, w_gate, w_up, w_down)
     late = jnp.concatenate([to_lanes(w) for w in late_names])
-    late_full = gather_shards(late, shards, core)
+    late_full, unused = gather_shards(late, shards, core + rest[:1], early_part)
 
     def unpack(full, shapes):
         outs, at = [], 0
@@ -487,7 +504,8 @@
         )
 
     ways = [rest + across, across + rest]
-    feed_sum = reduce_shards(pack_grads((wgate_grad, wup_grad, down_grad)), shards, core, ways)
+    feed = Reduction(pack_grads((wgate_grad, wup_grad, down_grad)), shards, core, ways)
+    feed_first = feed.first_stage()
 
     hidden_grad = right_product(gate_grad, feed_gate) + right_product(upper_grad, feed_up)
     unused, norm_pull = jax.vjp(rms_norm, after_two, gain_three)
@@ -496,7 +514,10 @@
     cross_low = grad_two.astype(jnp.bfloat16)
     cross_output_grad = left_matrix_product(attn_two, cross_low)
     attn_two_grad = right_product(cross_low, cross_out).astype(jnp.bfloat16)
-    cq_grad, enckey_term, encvalue_term = cross_backward(cross_q, enc_kv, attn_two_grad, probs_two)
+    cq_grad, enckey_term, encvalue_term = cross_backward(
+        cross_q, enc_kv, attn_two_grad, probs_two, feed_first
+    )
+    feed_across = feed.across_stage(slice(None))
     enc_sum = reduce_axis(jnp.concatenate([enckey_term, encvalue_term], axis=1), "ctx", ctxs)
     enc_low = enc_sum.astype(jnp.bfloat16)
     cquery_grad = left_matrix_product(hidden_two, cq_grad)
@@ -507,14 +528,26 @@
     self_low = grad_one.astype(jnp.bfloat16)
     sout_grad = left_matrix_product(attn_one, self_low)
     attn_one_grad = right_product(self_low, self_out).astype(jnp.bfloat16)
-    query_grad, key_term, value_term, line_grad = self_backward(
-        all_blk, my_blk, query, kv, attn_one_grad, probs_one
-    )
-    kv_sum = reduce_axis(jnp.concatenate([key_term, value_term], axis=1), "ctx", ctxs)
+    enc_weight_grad = left_matrix_product(encoder, enc_low)
+    cross_pack = pack_grads((cquery_grad, enc_weight_grad, cross_output_grad))
+    cross = Reduction(cross_pack, shards, core, ways)
+    operands = (all_blk, my_blk, query, kv, attn_one_grad, probs_one)
+    pair_grads = [self_backward(0, *operands, (feed_across,))]
+    feed_shard = feed.shard_stage()
+    cross_first = cross.first_stage()
+    pair_grads.append(self_backward(1, *operands, (pair_grads[0][0], feed_shard, cross_first)))
+    cross_across = cross.across_stage(slice(None))
+    feed_sum = feed.back_stage()
+    pair_grads.append(self_backward(2, *operands, (pair_grads[1][0], cross_across)))
+    dqs, dks, dvs, dts = zip(*pair_grads)
+    query_grad = jnp.concatenate(dqs, axis=1)
+    line_grad = jnp.concatenate(dts, axis=0)
+    kv_sum = reduce_axis(jnp.concatenate(dks + dvs, axis=1), "ctx", ctxs)
+    cross.shard_stage()
+    cross_sum = cross.back_stage()
     kv_low = kv_sum.astype(jnp.bfloat16)
 
     encoder_grad = right_product(enc_low, cross_kv_weight)
-    enc_weight_grad = left_matrix_product(encoder, enc_low)
     squery_grad = left_matrix_product(hidden_first_layer, query_grad)
     kv_weight_grad = left_matrix_product(hidden_first_layer, kv_low)
     hidden_grad = right_product(query_grad, self_query) + right_product(kv_low, self_kv_weight)
@@ -535,12 +568,16 @@
     small_pack = jnp.pad(small_pack, ((0, 0), (0, pad_rows - small_pack.shape[1]), (0, 0)))
     attn_pack = jnp.concatenate(
         [
-            pack_grads((squery_grad, kv_weight_grad, sout_grad, cquery_grad, enc_weight_grad, cross_output_grad)),
+            pack_grads((squery_grad, kv_weight_grad, sout_grad)),
             small_pack.astype(jnp.bfloat16),
         ],
         axis=1,
     )
-    attn_sum = reduce_shards(attn_pack, shards, core, ways)
+    attn = Reduction(attn_pack, shards, core, ways)
+    attn.first_stage()
+    attn.across_stage(slice(None))
+    attn.shard_stage()
+    attn_sum = attn.back_stage()
 
     def unpack_sum(total, shapes):
         outs, at = [], 0
@@ -552,9 +589,11 @@
 
     (g_gate, g_up, g_down), unused = unpack_sum(feed_sum, [w_gate.shape, w_up.shape, w_down.shape])
     own = width // shards
-    (g_query, g_kv, g_out, g_cquery, g_enc, g_cout), at = unpack_sum(
-        attn_sum,
-        [w_query.shape, (own, 2 * inner), w_out.shape, c_query.shape, (own, 2 * inner), c_out.shape],
+    (g_cquery, g_enc, g_cout), unused = unpack_sum(
+        cross_sum, [c_query.shape, (own, 2 * inner), c_out.shape]
+    )
+    (g_query, g_kv, g_out), at = unpack_sum(
+        attn_sum, [w_query.shape, (own, 2 * inner), w_out.shape]
     )
     tail = attn_sum[at:].astype(jnp.float32)
     g_gains = [tail[i * small_rows : (i + 1) * small_rows].reshape(-1) for i in range(3)]

time: 346 us -> 346 us (level)
  local copies, waits for them, and re-layouts: 62.5 us -> 45.6 us
  starting transfers between devices: 74.1 us -> 90.2 us
  Pallas kernels: 48.5 us -> 53 us
    ppermute x45 -> x63, starting transfers between devices: 74.1 us -> 90.2 us  [swap(): return lax.ppermute(value, axis, [(i, i ^ bit) for i in range(size)])]
    unnamed x203 -> x250, local copies, waits for them, and re-layouts: 48.1 us -> 35.1 us
    dot_general x9, matrix products: 11.3 us -> 5.04 us  [left_matrix_product(): lax.dot_general(left, right, (((0,), (0,)), ((), ())), preferred_element_...]
    pallas_call x1 -> x3, Pallas kernels: 19 us -> 22.2 us  [self_backward(): pl.pallas_call(functools.partial(self_backward_kernel, len(ties)), grid=(...]
    ppermute x45 -> x63, waiting for transfers between devices: 97.4 us -> 95.4 us  [swap(): return lax.ppermute(value, axis, [(i, i ^ bit) for i in range(size)])]
  transfers between devices with their start and end apart: 45 -> 63, of which waited for: 20 -> 27; matrix products, arithmetic and copies ran while one was open for 20% -> 14% of each run, Pallas kernels for 6% -> 12%
where the time goes in v2:
time: 346 us; the launch traced here: 339 us
  waiting for transfers between devices  95.4 us (28%)
  starting transfers between devices  90.2 us (26%)
  Pallas kernels  53 us (15%)
  local copies, waits for them, and re-layouts  45.6 us (13%)
  matrix products  26 us (8%)
  other arithmetic  25.5 us (7%)
    ppermute x63, waiting for transfers between devices, swap(): return lax.ppermute(value, axis, [(i, i ^ bit) for i in range(size)])  95.4 us
    ppermute x63, starting transfers between devices, swap(): return lax.ppermute(value, axis, [(i, i ^ bit) for i in range(size)])  90.2 us
    unnamed x250, local copies, waits for them, and re-layouts  35.1 us
    pallas_call x3, Pallas kernels, self_backward(): pl.pallas_call(functools.partial(self_backward_kernel, len(ties)), grid=(...  22.2 us
    pallas_call x1, Pallas kernels, self_forward(): pl.pallas_call(self_forward_kernel, grid=(PAIRS,), in_specs=[scalars, sca...  19.3 us
    dot_general x9, matrix products, right_product(): lax.dot_general(left, right, (((1,), (1,)), ((), ())), preferred_element_...  13.1 us
    pallas_call x1, Pallas kernels, cross_backward(): pl.pallas_call(cross_backward_kernel, grid=(PAIRS,), in_specs=[column(row...  7.41 us
    dot_general x9, matrix products, product(): return jnp.dot(left, right, preferred_element_type=jnp.float32)  7.1 us
  transfers between devices with their start and end apart: 63, of which 27 were waited for; matrix products, arithmetic and copies ran while one was open for 14% of the time, Pallas kernels for 12%

profile of v2, /device:TPU:1, one launch (start us, length us, event | category | flops | bytes accessed | tf_op | source)
XLA Modules:
  0.0 339.1 jit_solution(1713877551500753)
XLA Ops:
  14.0 2.1 collective-permute-start.1
  16.1 2.3 collective-permute-start.2
  32.4 3.2 collective-permute-start.8
  37.7 4.5 %collective-permute-done.7 = bf16[1056,128]{1,0:T(8,128)(2,1)S(1)} collective-permute-done((bf16[1056,128]{1,0:T(8,128)(2,1)S(1)}, bf16[1056,128]{1,0:T(8,128)(2,1)S(1)}, u32[]{:S(2)}, u32[]{:S(2)}) %collective-permute-start.7) | collective-permute-done | bytes 270368 | tf_op jit(solution)/shard_map/ppermute | solution.py:55
  42.4 9.6 %collective-permute-done.9 = bf16[1056,128]{1,0:T(8,128)(2,1)S(1)} collective-permute-done((bf16[1056,128]{1,0:T(8,128)(2,1)S(1)}, bf16[1056,128]{1,0:T(8,128)(2,1)S(1)}, u32[]{:S(2)}, u32[]{:S(2)}) %collective-permute-start.9) | collective-permute-done | bytes 270368 | tf_op jit(solution)/shard_map/ppermute | solution.py:55
  53.7 7.7 %collective-permute-done.4 = bf16[4,488,128]{2,1,0:T(8,128)(2,1)S(1)} collective-permute-done((bf16[4,488,128]{2,1,0:T(8,128)(2,1)S(1)}, bf16[4,488,128]{2,1,0:T(8,128)(2,1)S(1)}, u32[]{:S(2)}, u32[]{:S(2)}) %collective-permute-start.4) | collective-permute-done | bytes 499744 | tf_op jit(solution)/shard_map/ppermute | solution.py:55
  61.6 6.3 %collective-permute-start.5 = (bf16[4,976,128]{2,1,0:T(8,128)(2,1)S(1)}, bf16[4,976,128]{2,1,0:T(8,128)(2,1)S(1)}, u32[]{:S(2)}, u32[]{:S(2)}) collective-permute-start(bf16[4,976,128]{2,1,0:T(8,128)(2,1)S(1)} %pad_maximum_fusion.3), channel_id=1, source_target_pairs={{0,8},{8,0},{16,24},{24,16},{1,9},{9,1},{17,25},{25,17},{2,10},{10... | collective-permute-start | bytes 2998280 | tf_op jit(solution)/shard_map/ppermute | solution.py:55
  67.8 4.5 %collective-permute-done.10 = bf16[4,1056,128]{2,1,0:T(8,128)(2,1)S(1)} collective-permute-done((bf16[4,1056,128]{2,1,0:T(8,128)(2,1)S(1)}, bf16[4,1056,128]{2,1,0:T(8,128)(2,1)S(1)}, u32[]{:S(2)}, u32[]{:S(2)}) %collective-permute-start.10) | collective-permute-done | bytes 1081376 | tf_op jit(solution)/shard_map/ppermute | solution.py:55
  72.6 1.7 pad_maximum_fusion
  74.7 6.0 %collective-permute-start.11 = (bf16[4,2112,128]{2,1,0:T(8,128)(2,1)}, bf16[4,2112,128]{2,1,0:T(8,128)(2,1)}, u32[]{:S(2)}, u32[]{:S(2)}) collective-permute-start(bf16[4,2112,128]{2,1,0:T(8,128)(2,1)} %pad_maximum_fusion), channel_id=1, source_target_pairs={{0,8},{8,0},{16,24},{24,16},{1,9},{9,1},{17,25},{25,17},{2,10},{10... | collective-permute-start | bytes 6488072 | tf_op jit(solution)/shard_map/ppermute | solution.py:55
  81.5 1.6 convolution_convert_fusion.5
  87.5 23.5 %collective-permute-done.12 = bf16[256,768]{1,0:T(8,128)(2,1)S(1)} collective-permute-done((bf16[256,768]{1,0:T(8,128)(2,1)S(1)}, bf16[256,768]{1,0:T(8,128)(2,1)S(1)}, u32[]{:S(2)}, u32[]{:S(2)}) %collective-permute-start.12) | collective-permute-done | bytes 393248 | tf_op jit(solution)/shard_map/ppermute | solution.py:55
  111.1 1.5 broadcast_select_fusion.11
  112.7 19.3 %self_forward.1 = (bf16[512,384]{1,0:T(8,128)(2,1)S(1)}, bf16[6,512,1024]{2,1,0:T(8,128)(2,1)}) custom-call(s32[16]{0:T(128)S(1)} %pad_add_fusion.all_blk, s32[8]{0:T(128)S(1)} %and_select_fusion.my_blk, f32[6,1,2048]{2,1,0:T(1,128)S(1)} %broadcast_in_dim.74.w_ref, bf16[512,384]{1,0:T(8,128)(2,1)S(1)} %convolution_convert_fusion.14.q_ref, ...), custom_call_target="tpu_custom_call" | custom-call | flops 1610612736 | bytes 16777216 | tf_op jit(solution)/shard_map/self_forward/pallas_call | solution.py:306
  132.0 2.8 broadcast_select_fusion
  138.4 4.1 %cross_forward.1 = (bf16[512,384]{1,0:T(8,128)(2,1)S(1)}, bf16[6,512,512]{2,1,0:T(8,128)(2,1)S(1)}) custom-call(bf16[512,384]{1,0:T(8,128)(2,1)S(1)} %convolution_convert_fusion.13.q_ref, bf16[512,768]{1,0:T(8,128)(2,1)S(1)} %pad_maximum_fusion.6.k_ref.v_ref, bf16[512,768]{1,0:T(8,128)(2,1)S(1)} %pad_maximum_fusion.6.k_ref.v_ref), custom_call_target="tpu_custom_call" | custom-call | flops 805306368 | bytes 16777216 | tf_op jit(solution)/shard_map/cross_forward/pallas_call | solution.py:356
  146.8 2.6 fusion.7
  149.4 1.7 fusion.88
  154.4 1.7 broadcast_select_fusion.2
  157.0 1.6 fusion.15
  158.5 2.0 copy.80
  160.6 3.8 %multiply_reduce_fusion = (bf16[512]{0:T(512)(128)(2,1)}, f32[512]{0:T(512)S(1)}, f32[512,512]{0,1:T(8,128)S(1)}) fusion(f32[512,512]{0,1:T(8,128)} %copy-done.10, f32[512]{0:T(512)S(1)} %fusion.68, f32[512]{0:T(512)S(1)} %bitcast.286, f32[512,512]{0,1:T(8,128)} %fusion.88, bf16[512,1024]{1,0:T(8,128)(2,1)} %copy-done.35, bf16[512,1024]{1,0:T(8,128)(2,1)} %bitcast.222), kind=kOutput, calls=%fused_computation.72 | convolution fusion | flops 538704896 | bytes 5250048 | tf_op jit(solution)/shard_map/dot_general | solution.py:41
  167.4 2.2 add_convert_fusion.tie_ref
  169.7 7.4 %cross_backward.1 = (bf16[512,384]{1,0:T(8,128)(2,1)S(1)}, bf16[512,384]{1,0:T(8,128)(2,1)S(1)}, bf16[512,384]{1,0:T(8,128)(2,1)S(1)}) custom-call(bf16[512,384]{1,0:T(8,128)(2,1)S(1)} %convolution_convert_fusion.13.q_ref, bf16[512,768]{1,0:T(8,128)(2,1)S(1)} %pad_maximum_fusion.6.k_ref.v_ref, bf16[512,768]{1,0:T(8,128)(2,1)S(1)} %pad_maximum_fusion.6.k_ref.v_ref, ...), custom_call_target="tpu_custom_call" | custom-call | flops 1610612736 | bytes 16777216 | tf_op jit(solution)/shard_map/cross_backward/pallas_call | solution.py:370
  183.5 7.3 %collective-permute-done.55 = bf16[4,384,128]{2,1,0:T(8,128)(2,1)S(1)} collective-permute-done((bf16[4,384,128]{2,1,0:T(8,128)(2,1)S(1)}, bf16[4,384,128]{2,1,0:T(8,128)(2,1)S(1)}, u32[]{:S(2)}, u32[]{:S(2)}) %collective-permute-start.55) | collective-permute-done | bytes 393248 | tf_op jit(solution)/shard_map/ppermute | solution.py:55
  192.4 6.9 %collective-permute-done.19 = bf16[256,768]{1,0:T(8,128)(2,1)S(1)} collective-permute-done((bf16[256,768]{1,0:T(8,128)(2,1)S(1)}, bf16[256,768]{1,0:T(8,128)(2,1)S(1)}, u32[]{:S(2)}, u32[]{:S(2)}) %collective-permute-start.19) | collective-permute-done | bytes 393248 | tf_op jit(solution)/shard_map/ppermute | solution.py:55
  204.1 7.3 %self_backward.3 = (bf16[512,128]{1,0:T(8,128)(2,1)S(1)}, bf16[1024,128]{1,0:T(8,128)(2,1)S(1)}, bf16[1024,128]{1,0:T(8,128)(2,1)S(1)}, f32[2,1,2048]{2,1,0:T(1,128)S(1)}) custom-call(s32[16]{0:T(128)S(1)} %pad_add_fusion.all_blk, s32[8]{0:T(128)S(1)} %and_select_fusion.my_blk, bf16[512,384]{1,0:T(8,128)(2,1)S(1)} %convolution_convert_fusion.14.q_ref, ...), custom_call_target="tpu_custom_call" | custom-call | flops 1073741824 | bytes 16777216 | tf_op jit(solution)/shard_map/self_backward/pallas_call | solution.py:328
  211.6 2.7 collective-permute-start.59
  214.4 4.9 %collective-permute-start.58 = (bf16[192,128]{1,0:T(8,128)(2,1)S(1)}, bf16[192,128]{1,0:T(8,128)(2,1)S(1)}, u32[]{:S(2)}, u32[]{:S(2)}) collective-permute-start(bf16[192,128]{1,0:T(8,128)(2,1)S(1)} %get-tuple-element.235), channel_id=1, source_target_pairs={{0,4},{2,6},{4,0},{6,2},{1,5},{3,7},{5,1},{7,3},{8,12},{10,14},{12... | collective-permute-start | bytes 147464 | tf_op jit(solution)/shard_map/ppermute | solution.py:55
  219.5 2.1 collective-permute-start.18
  224.9 2.3 collective-permute-done.17
  231.3 2.8 collective-permute-done.54
  234.1 4.3 %collective-permute-start.62 = (bf16[1536,128]{1,0:T(8,128)(2,1)S(1)}, bf16[1536,128]{1,0:T(8,128)(2,1)S(1)}, u32[]{:S(2)}, u32[]{:S(2)}) collective-permute-start(bf16[1536,128]{1,0:T(8,128)(2,1)S(1)} %pad_maximum_fusion.19), channel_id=1, source_target_pairs={{0,8},{8,0},{16,24},{24,16},{1,9},{9,1},{17,25},{25,17},{2,10},{10... | collective-permute-start | bytes 1179656 | tf_op jit(solution)/shard_map/ppermute | solution.py:55
  239.3 7.5 %self_backward.4 = (bf16[512,128]{1,0:T(8,128)(2,1)S(1)}, bf16[1024,128]{1,0:T(8,128)(2,1)S(1)}, bf16[1024,128]{1,0:T(8,128)(2,1)S(1)}, f32[2,1,2048]{2,1,0:T(1,128)S(1)}) custom-call(s32[16]{0:T(128)S(1)} %pad_add_fusion.all_blk, s32[8]{0:T(128)S(1)} %and_select_fusion.my_blk, bf16[512,384]{1,0:T(8,128)(2,1)S(1)} %convolution_convert_fusion.14.q_ref, ...), custom_call_target="tpu_custom_call" | custom-call | flops 1073741824 | bytes 16777216 | tf_op jit(solution)/shard_map/self_backward/pallas_call | solution.py:328
  254.0 7.3 %self_backward.5 = (bf16[512,128]{1,0:T(8,128)(2,1)S(1)}, bf16[1024,128]{1,0:T(8,128)(2,1)S(1)}, bf16[1024,128]{1,0:T(8,128)(2,1)S(1)}, f32[2,1,2048]{2,1,0:T(1,128)S(1)}) custom-call(s32[16]{0:T(128)S(1)} %pad_add_fusion.all_blk, s32[8]{0:T(128)S(1)} %and_select_fusion.my_blk, bf16[512,384]{1,0:T(8,128)(2,1)S(1)} %convolution_convert_fusion.14.q_ref, ...), custom_call_target="tpu_custom_call" | custom-call | flops 1073741824 | bytes 16777216 | tf_op jit(solution)/shard_map/self_backward/pallas_call | solution.py:328
  261.4 1.4 fusion.89
  267.1 2.9 collective-permute-start.49
  270.9 2.9 collective-permute-start.42
  279.0 4.1 %collective-permute-done.43 = bf16[96,128]{1,0:T(8,128)(2,1)S(1)} collective-permute-done((bf16[96,128]{1,0:T(8,128)(2,1)S(1)}, bf16[96,128]{1,0:T(8,128)(2,1)S(1)}, u32[]{:S(2)}, u32[]{:S(2)}) %collective-permute-start.43) | collective-permute-done | bytes 24608 | tf_op jit(solution)/shard_map/ppermute | solution.py:55
  284.2 1.9 collective-permute-done.44
  286.3 4.0 %collective-permute-start.52 = (bf16[768,128]{1,0:T(8,128)(2,1)S(1)}, bf16[768,128]{1,0:T(8,128)(2,1)S(1)}, u32[]{:S(2)}, u32[]{:S(2)}) collective-permute-start(bf16[768,128]{1,0:T(8,128)(2,1)S(1)} %pad_maximum_fusion.21), channel_id=1, source_target_pairs={{0,8},{8,0},{16,24},{24,16},{1,9},{9,1},{17,25},{25,17},{2,10},{10... | collective-permute-start | bytes 589832 | tf_op jit(solution)/shard_map/ppermute | solution.py:55
  301.3 4.4 %collective-permute-done.25 = bf16[4,200,128]{2,1,0:T(8,128)(2,1)S(1)} collective-permute-done((bf16[4,200,128]{2,1,0:T(8,128)(2,1)S(1)}, bf16[4,200,128]{2,1,0:T(8,128)(2,1)S(1)}, u32[]{:S(2)}, u32[]{:S(2)}) %collective-permute-start.25) | collective-permute-done | bytes 204832 | tf_op jit(solution)/shard_map/ppermute | solution.py:55
  308.2 1.9 collective-permute-done.33
  310.2 2.9 collective-permute-start.36
  313.9 2.9 collective-permute-start.29
  318.7 1.8 collective-permute-done.28
  325.0 1.8 collective-permute-done.31
  326.8 6.7 %collective-permute-start.39 = (bf16[800,128]{1,0:T(8,128)(2,1)S(1)}, bf16[800,128]{1,0:T(8,128)(2,1)S(1)}, u32[]{:S(2)}, u32[]{:S(2)}) collective-permute-start(bf16[800,128]{1,0:T(8,128)(2,1)S(1)} %pad_maximum_fusion.20), channel_id=1, source_target_pairs={{0,8},{8,0},{16,24},{24,16},{1,9},{9,1},{17,25},{25,17},{2,10},{10... | collective-permute-start | bytes 614408 | tf_op jit(solution)/shard_map/ppermute | solution.py:55
  (520 shorter events, 117.0 us)
Async XLA Ops:
  14.0 21.8 %collective-permute-start.1 = (bf16[488,128]{1,0:T(8,128)(2,1)}, bf16[488,128]{1,0:T(8,128)(2,1)}, u32[]{:S(2)}, u32[]{:S(2)}) collective-permute-start(bf16[488,128]{1,0:T(8,128)(2,1)} %get-tuple-element.119), channel_id=1, source_target_pairs={{0,2},{2,0},{4,6},{6,4},{1,3},{3,1},{5,7},{7,5},{8,10},{10,8},{12,... | collective-permute-start | bytes 374792 | tf_op jit(solution)/shard_map/ppermute | solution.py:55
  16.1 20.7 %collective-permute-start.2 = (bf16[488,128]{1,0:T(8,128)(2,1)}, bf16[488,128]{1,0:T(8,128)(2,1)}, u32[]{:S(2)}, u32[]{:S(2)}) collective-permute-start(bf16[488,128]{1,0:T(8,128)(2,1)} %get-tuple-element.119), channel_id=1, source_target_pairs={{0,4},{2,6},{4,0},{6,2},{1,5},{3,7},{5,1},{7,3},{8,12},{10,14},{12... | collective-permute-start | bytes 374792 | tf_op jit(solution)/shard_map/ppermute | solution.py:55
  18.4 13.6 %collective-permute-start.3 = (bf16[488,128]{1,0:T(8,128)(2,1)}, bf16[488,128]{1,0:T(8,128)(2,1)S(1)}, u32[]{:S(2)}, u32[]{:S(2)}) collective-permute-start(bf16[488,128]{1,0:T(8,128)(2,1)} %get-tuple-element.119), channel_id=1, source_target_pairs={{0,6},{2,4},{4,2},{6,0},{1,7},{3,5},{5,3},{7,1},{8,14},{10,12},{12... | collective-permute-start | bytes 374792 | tf_op jit(solution)/shard_map/ppermute | solution.py:55
  19.2 34.4 %collective-permute-start = (s32[8]{0:T(128)S(1)}, s32[8]{0:T(128)S(1)}, u32[]{:S(2)}, u32[]{:S(2)}) collective-permute-start(s32[8]{0:T(128)S(1)} %and_select_fusion.my_blk), channel_id=1, source_target_pairs={{0,1},{1,0},{2,3},{3,2},{4,5},{5,4},{6,7},{7,6},{8,9},{9,8},{10,11... | collective-permute-start | bytes 104 | tf_op jit(solution)/shard_map/ppermute | solution.py:55
  32.0 10.3 %collective-permute-start.7 = (bf16[1056,128]{1,0:T(8,128)(2,1)S(1)}, bf16[1056,128]{1,0:T(8,128)(2,1)S(1)}, u32[]{:S(2)}, u32[]{:S(2)}) collective-permute-start(bf16[1056,128]{1,0:T(8,128)(2,1)S(1)} %slice_select_fusion.1), channel_id=1, source_target_pairs={{0,2},{2,0},{4,6},{6,4},{1,3},{3,1},{5,7},{7,5},{8,10},{10,8},{12,... | collective-permute-start | bytes 811016 | tf_op jit(solution)/shard_map/ppermute | solution.py:55
  32.4 9.9 %collective-permute-start.8 = (bf16[1056,128]{1,0:T(8,128)(2,1)S(1)}, bf16[1056,128]{1,0:T(8,128)(2,1)S(1)}, u32[]{:S(2)}, u32[]{:S(2)}) collective-permute-start(bf16[1056,128]{1,0:T(8,128)(2,1)S(1)} %slice_select_fusion.1), channel_id=1, source_target_pairs={{0,4},{2,6},{4,0},{6,2},{1,5},{3,7},{5,1},{7,3},{8,12},{10,14},{12... | collective-permute-start | bytes 811016 | tf_op jit(solution)/shard_map/ppermute | solution.py:55
  35.8 16.1 %collective-permute-start.9 = (bf16[1056,128]{1,0:T(8,128)(2,1)S(1)}, bf16[1056,128]{1,0:T(8,128)(2,1)S(1)}, u32[]{:S(2)}, u32[]{:S(2)}) collective-permute-start(bf16[1056,128]{1,0:T(8,128)(2,1)S(1)} %slice_select_fusion.1), channel_id=1, source_target_pairs={{0,6},{2,4},{4,2},{6,0},{1,7},{3,5},{5,3},{7,1},{8,14},{10,12},{12... | collective-permute-start | bytes 811016 | tf_op jit(solution)/shard_map/ppermute | solution.py:55
  52.0 20.4 %collective-permute-start.10 = (bf16[4,1056,128]{2,1,0:T(8,128)(2,1)S(1)}, bf16[4,1056,128]{2,1,0:T(8,128)(2,1)S(1)}, u32[]{:S(2)}, u32[]{:S(2)}) collective-permute-start(bf16[4,1056,128]{2,1,0:T(8,128)(2,1)S(1)} %bitcast_dynamic-update-slice_fusion), channel_id=1, source_target_pairs={{0,16},{8,24},{16,0},{24,8},{1,17},{9,25},{17,1},{25,9},{2,18},{10... | collective-permute-start | bytes 3244040 | tf_op jit(solution)/shard_map/ppermute | solution.py:55
  53.3 8.1 %collective-permute-start.4 = (bf16[4,488,128]{2,1,0:T(8,128)(2,1)S(1)}, bf16[4,488,128]{2,1,0:T(8,128)(2,1)S(1)}, u32[]{:S(2)}, u32[]{:S(2)}) collective-permute-start(bf16[4,488,128]{2,1,0:T(8,128)(2,1)S(1)} %bitcast_dynamic-update-slice_fusion.4), channel_id=1, source_target_pairs={{0,1},{1,0},{2,3},{3,2},{4,5},{5,4},{6,7},{7,6},{8,9},{9,8},{10,11... | collective-permute-start | bytes 1499144 | tf_op jit(solution)/shard_map/ppermute | solution.py:55
  61.6 19.2 %collective-permute-start.5 = (bf16[4,976,128]{2,1,0:T(8,128)(2,1)S(1)}, bf16[4,976,128]{2,1,0:T(8,128)(2,1)S(1)}, u32[]{:S(2)}, u32[]{:S(2)}) collective-permute-start(bf16[4,976,128]{2,1,0:T(8,128)(2,1)S(1)} %pad_maximum_fusion.3), channel_id=1, source_target_pairs={{0,8},{8,0},{16,24},{24,16},{1,9},{9,1},{17,25},{25,17},{2,10},{10... | collective-permute-start | bytes 2998280 | tf_op jit(solution)/shard_map/ppermute | solution.py:55
  74.7 57.3 %collective-permute-start.11 = (bf16[4,2112,128]{2,1,0:T(8,128)(2,1)}, bf16[4,2112,128]{2,1,0:T(8,128)(2,1)}, u32[]{:S(2)}, u32[]{:S(2)}) collective-permute-start(bf16[4,2112,128]{2,1,0:T(8,128)(2,1)} %pad_maximum_fusion), channel_id=1, source_target_pairs={{0,8},{8,0},{16,24},{24,16},{1,9},{9,1},{17,25},{25,17},{2,10},{10... | collective-permute-start | bytes 6488072 | tf_op jit(solution)/shard_map/ppermute | solution.py:55
  83.2 27.9 %collective-permute-start.6 = (bf16[512,768]{1,0:T(8,128)(2,1)}, bf16[512,768]{1,0:T(8,128)(2,1)}, u32[]{:S(2)}, u32[]{:S(2)}) collective-permute-start(bf16[512,768]{1,0:T(8,128)(2,1)} %convolution_convert_fusion.5), channel_id=1, source_target_pairs={{0,1},{1,0},{2,3},{3,2},{4,5},{5,4},{6,7},{7,6},{8,9},{9,8},{10,11... | collective-permute-start | bytes 2359304 | tf_op jit(solution)/shard_map/ppermute | solution.py:55
  83.9 27.1 %collective-permute-start.12 = (bf16[256,768]{1,0:T(8,128)(2,1)S(1)}, bf16[256,768]{1,0:T(8,128)(2,1)S(1)}, u32[]{:S(2)}, u32[]{:S(2)}) collective-permute-start(bf16[256,768]{1,0:T(8,128)(2,1)S(1)} %fusion.16), channel_id=1, source_target_pairs={{0,1},{1,0},{2,3},{3,2},{4,5},{5,4},{6,7},{7,6},{8,9},{9,8},{10,11... | collective-permute-start | bytes 1179656 | tf_op jit(solution)/shard_map/ppermute | solution.py:55
  156.2 10.6 %collective-permute-start.13 = (bf16[4,1536,128]{2,1,0:T(8,128)(2,1)}, bf16[4,1536,128]{2,1,0:T(8,128)(2,1)}, u32[]{:S(2)}, u32[]{:S(2)}) collective-permute-start(bf16[4,1536,128]{2,1,0:T(8,128)(2,1)} %broadcast_select_fusion.2), channel_id=1, source_target_pairs={{0,8},{8,0},{16,24},{24,16},{1,9},{9,1},{17,25},{25,17},{2,10},{10... | collective-permute-start | bytes 4718600 | tf_op jit(solution)/shard_map/ppermute | solution.py:55
  180.0 10.8 %collective-permute-start.55 = (bf16[4,384,128]{2,1,0:T(8,128)(2,1)S(1)}, bf16[4,384,128]{2,1,0:T(8,128)(2,1)S(1)}, u32[]{:S(2)}, u32[]{:S(2)}) collective-permute-start(bf16[4,384,128]{2,1,0:T(8,128)(2,1)S(1)} %get-tuple-element.148), channel_id=1, source_target_pairs={{0,1},{1,0},{2,3},{3,2},{4,5},{5,4},{6,7},{7,6},{8,9},{9,8},{10,11... | collective-permute-start | bytes 1179656 | tf_op jit(solution)/shard_map/ppermute | solution.py:55
  180.3 10.5 %collective-permute-start.14 = (bf16[4,384,128]{2,1,0:T(8,128)(2,1)S(1)}, bf16[4,384,128]{2,1,0:T(8,128)(2,1)S(1)}, u32[]{:S(2)}, u32[]{:S(2)}) collective-permute-start(bf16[4,384,128]{2,1,0:T(8,128)(2,1)S(1)} %get-tuple-element.149), channel_id=1, source_target_pairs={{0,16},{8,24},{16,0},{24,8},{1,17},{9,25},{17,1},{25,9},{2,18},{10... | collective-permute-start | bytes 1179656 | tf_op jit(solution)/shard_map/ppermute | solution.py:55
  181.7 17.6 %collective-permute-start.19 = (bf16[256,768]{1,0:T(8,128)(2,1)S(1)}, bf16[256,768]{1,0:T(8,128)(2,1)S(1)}, u32[]{:S(2)}, u32[]{:S(2)}) collective-permute-start(bf16[256,768]{1,0:T(8,128)(2,1)S(1)} %broadcast_select_fusion.18), channel_id=1, source_target_pairs={{0,1},{1,0},{2,3},{3,2},{4,5},{5,4},{6,7},{7,6},{8,9},{9,8},{10,11... | collective-permute-start | bytes 1179656 | tf_op jit(solution)/shard_map/ppermute | solution.py:55
  191.1 12.9 %collective-permute-start.15 = (bf16[4,192,128]{2,1,0:T(8,128)(2,1)S(1)}, bf16[4,192,128]{2,1,0:T(8,128)(2,1)S(1)}, u32[]{:S(2)}, u32[]{:S(2)}) collective-permute-start(bf16[4,192,128]{2,1,0:T(8,128)(2,1)S(1)} %broadcast_select_fusion.30), channel_id=1, source_target_pairs={{0,1},{1,0},{2,3},{3,2},{4,5},{5,4},{6,7},{7,6},{8,9},{9,8},{10,11... | collective-permute-start | bytes 589832 | tf_op jit(solution)/shard_map/ppermute | solution.py:55
  200.2 38.1 %collective-permute-start.20 = (bf16[4,768,128]{2,1,0:T(8,128)(2,1)S(1)}, bf16[4,768,128]{2,1,0:T(8,128)(2,1)S(1)}, u32[]{:S(2)}, u32[]{:S(2)}) collective-permute-start(bf16[4,768,128]{2,1,0:T(8,128)(2,1)S(1)} %broadcast_select_fusion.8), channel_id=1, source_target_pairs={{0,8},{8,0},{16,24},{24,16},{1,9},{9,1},{17,25},{25,17},{2,10},{10... | collective-permute-start | bytes 2359304 | tf_op jit(solution)/shard_map/ppermute | solution.py:55
  201.5 10.0 %collective-permute-start.56 = (bf16[4,192,128]{2,1,0:T(8,128)(2,1)S(1)}, bf16[4,192,128]{2,1,0:T(8,128)(2,1)S(1)}, u32[]{:S(2)}, u32[]{:S(2)}) collective-permute-start(bf16[4,192,128]{2,1,0:T(8,128)(2,1)S(1)} %broadcast_select_fusion.27), channel_id=1, source_target_pairs={{0,16},{8,24},{16,0},{24,8},{1,17},{9,25},{17,1},{25,9},{2,18},{10... | collective-permute-start | bytes 589832 | tf_op jit(solution)/shard_map/ppermute | solution.py:55
  211.6 10.1 %collective-permute-start.59 = (bf16[192,128]{1,0:T(8,128)(2,1)S(1)}, bf16[192,128]{1,0:T(8,128)(2,1)S(1)}, u32[]{:S(2)}, u32[]{:S(2)}) collective-permute-start(bf16[192,128]{1,0:T(8,128)(2,1)S(1)} %get-tuple-element.234), channel_id=1, source_target_pairs={{0,6},{2,4},{4,2},{6,0},{1,7},{3,5},{5,3},{7,1},{8,14},{10,12},{12... | collective-permute-start | bytes 147464 | tf_op jit(solution)/shard_map/ppermute | solution.py:55
  214.4 7.8 %collective-permute-start.58 = (bf16[192,128]{1,0:T(8,128)(2,1)S(1)}, bf16[192,128]{1,0:T(8,128)(2,1)S(1)}, u32[]{:S(2)}, u32[]{:S(2)}) collective-permute-start(bf16[192,128]{1,0:T(8,128)(2,1)S(1)} %get-tuple-element.235), channel_id=1, source_target_pairs={{0,4},{2,6},{4,0},{6,2},{1,5},{3,7},{5,1},{7,3},{8,12},{10,14},{12... | collective-permute-start | bytes 147464 | tf_op jit(solution)/shard_map/ppermute | solution.py:55
  219.3 4.1 %collective-permute-start.57 = (bf16[192,128]{1,0:T(8,128)(2,1)S(1)}, bf16[192,128]{1,0:T(8,128)(2,1)S(1)}, u32[]{:S(2)}, u32[]{:S(2)}) collective-permute-start(bf16[192,128]{1,0:T(8,128)(2,1)S(1)} %get-tuple-element.233), channel_id=1, source_target_pairs={{0,2},{2,0},{4,6},{6,4},{1,3},{3,1},{5,7},{7,5},{8,10},{10,8},{12,... | collective-permute-start | bytes 147464 | tf_op jit(solution)/shard_map/ppermute | solution.py:55
  219.5 5.3 %collective-permute-start.18 = (bf16[192,128]{1,0:T(8,128)(2,1)S(1)}, bf16[192,128]{1,0:T(8,128)(2,1)S(1)}, u32[]{:S(2)}, u32[]{:S(2)}) collective-permute-start(bf16[192,128]{1,0:T(8,128)(2,1)S(1)} %get-tuple-element.249), channel_id=1, source_target_pairs={{0,6},{2,4},{4,2},{6,0},{1,7},{3,5},{5,3},{7,1},{8,14},{10,12},{12... | collective-permute-start | bytes 147464 | tf_op jit(solution)/shard_map/ppermute | solution.py:55
  221.7 5.5 %collective-permute-start.17 = (bf16[192,128]{1,0:T(8,128)(2,1)S(1)}, bf16[192,128]{1,0:T(8,128)(2,1)S(1)}, u32[]{:S(2)}, u32[]{:S(2)}) collective-permute-start(bf16[192,128]{1,0:T(8,128)(2,1)S(1)} %get-tuple-element.250), channel_id=1, source_target_pairs={{0,4},{2,6},{4,0},{6,2},{1,5},{3,7},{5,1},{7,3},{8,12},{10,14},{12... | collective-permute-start | bytes 147464 | tf_op jit(solution)/shard_map/ppermute | solution.py:55
  222.2 5.0 %collective-permute-start.16 = (bf16[192,128]{1,0:T(8,128)(2,1)S(1)}, bf16[192,128]{1,0:T(8,128)(2,1)S(1)}, u32[]{:S(2)}, u32[]{:S(2)}) collective-permute-start(bf16[192,128]{1,0:T(8,128)(2,1)S(1)} %get-tuple-element.248), channel_id=1, source_target_pairs={{0,2},{2,0},{4,6},{6,4},{1,3},{3,1},{5,7},{7,5},{8,10},{10,8},{12,... | collective-permute-start | bytes 147464 | tf_op jit(solution)/shard_map/ppermute | solution.py:55
  223.4 4.1 %collective-permute-start.60 = (bf16[192,128]{1,0:T(8,128)(2,1)S(1)}, bf16[192,128]{1,0:T(8,128)(2,1)S(1)}, u32[]{:S(2)}, u32[]{:S(2)}) collective-permute-start(bf16[192,128]{1,0:T(8,128)(2,1)S(1)} %fusion.47), channel_id=1, source_target_pairs={{0,16},{8,24},{16,0},{24,8},{1,17},{9,25},{17,1},{25,9},{2,18},{10... | collective-permute-start | bytes 147464 | tf_op jit(solution)/shard_map/ppermute | solution.py:55
  234.1 12.7 %collective-permute-start.62 = (bf16[1536,128]{1,0:T(8,128)(2,1)S(1)}, bf16[1536,128]{1,0:T(8,128)(2,1)S(1)}, u32[]{:S(2)}, u32[]{:S(2)}) collective-permute-start(bf16[1536,128]{1,0:T(8,128)(2,1)S(1)} %pad_maximum_fusion.19), channel_id=1, source_target_pairs={{0,8},{8,0},{16,24},{24,16},{1,9},{9,1},{17,25},{25,17},{2,10},{10... | collective-permute-start | bytes 1179656 | tf_op jit(solution)/shard_map/ppermute | solution.py:55
  238.8 11.1 %collective-permute-start.45 = (bf16[4,192,128]{2,1,0:T(8,128)(2,1)S(1)}, bf16[4,192,128]{2,1,0:T(8,128)(2,1)S(1)}, u32[]{:S(2)}, u32[]{:S(2)}) collective-permute-start(bf16[4,192,128]{2,1,0:T(8,128)(2,1)S(1)} %get-tuple-element.187), channel_id=1, source_target_pairs={{0,1},{1,0},{2,3},{3,2},{4,5},{5,4},{6,7},{7,6},{8,9},{9,8},{10,11... | collective-permute-start | bytes 589832 | tf_op jit(solution)/shard_map/ppermute | solution.py:55
  239.0 10.9 %collective-permute-start.21 = (bf16[4,192,128]{2,1,0:T(8,128)(2,1)S(1)}, bf16[4,192,128]{2,1,0:T(8,128)(2,1)S(1)}, u32[]{:S(2)}, u32[]{:S(2)}) collective-permute-start(bf16[4,192,128]{2,1,0:T(8,128)(2,1)S(1)} %get-tuple-element.188), channel_id=1, source_target_pairs={{0,16},{8,24},{16,0},{24,8},{1,17},{9,25},{17,1},{25,9},{2,18},{10... | collective-permute-start | bytes 589832 | tf_op jit(solution)/shard_map/ppermute | solution.py:55
  250.1 3.8 %collective-permute-start.22 = (bf16[4,96,128]{2,1,0:T(8,128)(2,1)S(1)}, bf16[4,96,128]{2,1,0:T(8,128)(2,1)S(1)}, u32[]{:S(2)}, u32[]{:S(2)}) collective-permute-start(bf16[4,96,128]{2,1,0:T(8,128)(2,1)S(1)} %broadcast_select_fusion.38), channel_id=1, source_target_pairs={{0,1},{1,0},{2,3},{3,2},{4,5},{5,4},{6,7},{7,6},{8,9},{9,8},{10,11... | collective-permute-start | bytes 294920 | tf_op jit(solution)/shard_map/ppermute | solution.py:55
  251.3 15.7 %collective-permute-start.46 = (bf16[4,96,128]{2,1,0:T(8,128)(2,1)S(1)}, bf16[4,96,128]{2,1,0:T(8,128)(2,1)S(1)}, u32[]{:S(2)}, u32[]{:S(2)}) collective-permute-start(bf16[4,96,128]{2,1,0:T(8,128)(2,1)S(1)} %broadcast_select_fusion.37), channel_id=1, source_target_pairs={{0,16},{8,24},{16,0},{24,8},{1,17},{9,25},{17,1},{25,9},{2,18},{10... | collective-permute-start | bytes 294920 | tf_op jit(solution)/shard_map/ppermute | solution.py:55
  264.7 26.8 %collective-permute-start.23 = (bf16[512,768]{1,0:T(8,128)(2,1)}, bf16[512,768]{1,0:T(8,128)(2,1)}, u32[]{:S(2)}, u32[]{:S(2)}) collective-permute-start(bf16[512,768]{1,0:T(8,128)(2,1)} %broadcast_select_fusion.9), channel_id=1, source_target_pairs={{0,1},{1,0},{2,3},{3,2},{4,5},{5,4},{6,7},{7,6},{8,9},{9,8},{10,11... | collective-permute-start | bytes 2359304 | tf_op jit(solution)/shard_map/ppermute | solution.py:55
  267.1 6.7 %collective-permute-start.49 = (bf16[96,128]{1,0:T(8,128)(2,1)S(1)}, bf16[96,128]{1,0:T(8,128)(2,1)S(1)}, u32[]{:S(2)}, u32[]{:S(2)}) collective-permute-start(bf16[96,128]{1,0:T(8,128)(2,1)S(1)} %get-tuple-element.273), channel_id=1, source_target_pairs={{0,6},{2,4},{4,2},{6,0},{1,7},{3,5},{5,3},{7,1},{8,14},{10,12},{12... | collective-permute-start | bytes 73736 | tf_op jit(solution)/shard_map/ppermute | solution.py:55
  270.1 4.9 %collective-permute-start.47 = (bf16[96,128]{1,0:T(8,128)(2,1)S(1)}, bf16[96,128]{1,0:T(8,128)(2,1)S(1)}, u32[]{:S(2)}, u32[]{:S(2)}) collective-permute-start(bf16[96,128]{1,0:T(8,128)(2,1)S(1)} %get-tuple-element.272), channel_id=1, source_target_pairs={{0,2},{2,0},{4,6},{6,4},{1,3},{3,1},{5,7},{7,5},{8,10},{10,8},{12,... | collective-permute-start | bytes 73736 | tf_op jit(solution)/shard_map/ppermute | solution.py:55
  270.9 5.1 %collective-permute-start.42 = (bf16[96,128]{1,0:T(8,128)(2,1)S(1)}, bf16[96,128]{1,0:T(8,128)(2,1)S(1)}, u32[]{:S(2)}, u32[]{:S(2)}) collective-permute-start(bf16[96,128]{1,0:T(8,128)(2,1)S(1)} %get-tuple-element.268), channel_id=1, source_target_pairs={{0,6},{2,4},{4,2},{6,0},{1,7},{3,5},{5,3},{7,1},{8,14},{10,12},{12... | collective-permute-start | bytes 73736 | tf_op jit(solution)/shard_map/ppermute | solution.py:55
  277.4 5.8 %collective-permute-start.43 = (bf16[96,128]{1,0:T(8,128)(2,1)S(1)}, bf16[96,128]{1,0:T(8,128)(2,1)S(1)}, u32[]{:S(2)}, u32[]{:S(2)}) collective-permute-start(bf16[96,128]{1,0:T(8,128)(2,1)S(1)} %fusion.62), channel_id=1, source_target_pairs={{0,1},{1,0},{2,3},{3,2},{4,5},{5,4},{6,7},{7,6},{8,9},{9,8},{10,11... | collective-permute-start | bytes 73736 | tf_op jit(solution)/shard_map/ppermute | solution.py:55
  278.1 6.1 %collective-permute-start.51 = (bf16[192,128]{1,0:T(8,128)(2,1)S(1)}, bf16[192,128]{1,0:T(8,128)(2,1)S(1)}, u32[]{:S(2)}, u32[]{:S(2)}) collective-permute-start(bf16[192,128]{1,0:T(8,128)(2,1)S(1)} %pad_maximum_fusion.28), channel_id=1, source_target_pairs={{0,1},{1,0},{2,3},{3,2},{4,5},{5,4},{6,7},{7,6},{8,9},{9,8},{10,11... | collective-permute-start | bytes 147464 | tf_op jit(solution)/shard_map/ppermute | solution.py:55
  286.3 5.1 %collective-permute-start.52 = (bf16[768,128]{1,0:T(8,128)(2,1)S(1)}, bf16[768,128]{1,0:T(8,128)(2,1)S(1)}, u32[]{:S(2)}, u32[]{:S(2)}) collective-permute-start(bf16[768,128]{1,0:T(8,128)(2,1)S(1)} %pad_maximum_fusion.21), channel_id=1, source_target_pairs={{0,8},{8,0},{16,24},{24,16},{1,9},{9,1},{17,25},{25,17},{2,10},{10... | collective-permute-start | bytes 589832 | tf_op jit(solution)/shard_map/ppermute | solution.py:55
  299.1 6.6 %collective-permute-start.25 = (bf16[4,200,128]{2,1,0:T(8,128)(2,1)S(1)}, bf16[4,200,128]{2,1,0:T(8,128)(2,1)S(1)}, u32[]{:S(2)}, u32[]{:S(2)}) collective-permute-start(bf16[4,200,128]{2,1,0:T(8,128)(2,1)S(1)} %get-tuple-element.181), channel_id=1, source_target_pairs={{0,16},{8,24},{16,0},{24,8},{1,17},{9,25},{17,1},{25,9},{2,18},{10... | collective-permute-start | bytes 614408 | tf_op jit(solution)/shard_map/ppermute | solution.py:55
  300.1 6.2 %collective-permute-start.32 = (bf16[4,200,128]{2,1,0:T(8,128)(2,1)S(1)}, bf16[4,200,128]{2,1,0:T(8,128)(2,1)S(1)}, u32[]{:S(2)}, u32[]{:S(2)}) collective-permute-start(bf16[4,200,128]{2,1,0:T(8,128)(2,1)S(1)} %get-tuple-element.182), channel_id=1, source_target_pairs={{0,1},{1,0},{2,3},{3,2},{4,5},{5,4},{6,7},{7,6},{8,9},{9,8},{10,11... | collective-permute-start | bytes 614408 | tf_op jit(solution)/shard_map/ppermute | solution.py:55
  307.1 6.7 %collective-permute-start.26 = (bf16[4,100,128]{2,1,0:T(8,128)(2,1)S(1)}, bf16[4,100,128]{2,1,0:T(8,128)(2,1)S(1)}, u32[]{:S(2)}, u32[]{:S(2)}) collective-permute-start(bf16[4,100,128]{2,1,0:T(8,128)(2,1)S(1)} %broadcast_select_fusion.32), channel_id=1, source_target_pairs={{0,1},{1,0},{2,3},{3,2},{4,5},{5,4},{6,7},{7,6},{8,9},{9,8},{10,11... | collective-permute-start | bytes 307208 | tf_op jit(solution)/shard_map/ppermute | solution.py:55
  310.2 6.6 %collective-permute-start.36 = (bf16[100,128]{1,0:T(8,128)(2,1)S(1)}, bf16[100,128]{1,0:T(8,128)(2,1)S(1)}, u32[]{:S(2)}, u32[]{:S(2)}) collective-permute-start(bf16[100,128]{1,0:T(8,128)(2,1)S(1)} %get-tuple-element.255), channel_id=1, source_target_pairs={{0,6},{2,4},{4,2},{6,0},{1,7},{3,5},{5,3},{7,1},{8,14},{10,12},{12... | collective-permute-start | bytes 76808 | tf_op jit(solution)/shard_map/ppermute | solution.py:55
  313.1 4.4 %collective-permute-start.35 = (bf16[100,128]{1,0:T(8,128)(2,1)S(1)}, bf16[100,128]{1,0:T(8,128)(2,1)S(1)}, u32[]{:S(2)}, u32[]{:S(2)}) collective-permute-start(bf16[100,128]{1,0:T(8,128)(2,1)S(1)} %get-tuple-element.256), channel_id=1, source_target_pairs={{0,4},{2,6},{4,0},{6,2},{1,5},{3,7},{5,1},{7,3},{8,12},{10,14},{12... | collective-permute-start | bytes 76808 | tf_op jit(solution)/shard_map/ppermute | solution.py:55
  313.2 4.4 %collective-permute-start.34 = (bf16[100,128]{1,0:T(8,128)(2,1)S(1)}, bf16[100,128]{1,0:T(8,128)(2,1)S(1)}, u32[]{:S(2)}, u32[]{:S(2)}) collective-permute-start(bf16[100,128]{1,0:T(8,128)(2,1)S(1)} %get-tuple-element.254), channel_id=1, source_target_pairs={{0,2},{2,0},{4,6},{6,4},{1,3},{3,1},{5,7},{7,5},{8,10},{10,8},{12,... | collective-permute-start | bytes 76808 | tf_op jit(solution)/shard_map/ppermute | solution.py:55
  313.9 4.8 %collective-permute-start.29 = (bf16[100,128]{1,0:T(8,128)(2,1)S(1)}, bf16[100,128]{1,0:T(8,128)(2,1)S(1)}, u32[]{:S(2)}, u32[]{:S(2)}) collective-permute-start(bf16[100,128]{1,0:T(8,128)(2,1)S(1)} %get-tuple-element.252), channel_id=1, source_target_pairs={{0,6},{2,4},{4,2},{6,0},{1,7},{3,5},{5,3},{7,1},{8,14},{10,12},{12... | collective-permute-start | bytes 76808 | tf_op jit(solution)/shard_map/ppermute | solution.py:55
  317.6 4.0 %collective-permute-start.37 = (bf16[100,128]{1,0:T(8,128)(2,1)S(1)}, bf16[100,128]{1,0:T(8,128)(2,1)S(1)}, u32[]{:S(2)}, u32[]{:S(2)}) collective-permute-start(bf16[100,128]{1,0:T(8,128)(2,1)S(1)} %fusion.53), channel_id=1, source_target_pairs={{0,16},{8,24},{16,0},{24,8},{1,17},{9,25},{17,1},{25,9},{2,18},{10... | collective-permute-start | bytes 76808 | tf_op jit(solution)/shard_map/ppermute | solution.py:55
  326.8 8.3 %collective-permute-start.39 = (bf16[800,128]{1,0:T(8,128)(2,1)S(1)}, bf16[800,128]{1,0:T(8,128)(2,1)S(1)}, u32[]{:S(2)}, u32[]{:S(2)}) collective-permute-start(bf16[800,128]{1,0:T(8,128)(2,1)S(1)} %pad_maximum_fusion.20), channel_id=1, source_target_pairs={{0,8},{8,0},{16,24},{24,16},{1,9},{9,1},{17,25},{25,17},{2,10},{10... | collective-permute-start | bytes 614408 | tf_op jit(solution)/shard_map/ppermute | solution.py:55
  (77 other events, 616.8 us)
